TPU v7x, 256 devices: a whole 4x4x8 slice. The times are simulated.
256 devices in a mesh: seq: 16 (over y_hi, z), inner: 8 (over x, core), chan: 2 (over y_lo).
Axes of the slice: x: 4, y: 4 (y_hi: 2, y_lo: 2; y = y_hi * 2 + y_lo), z: 8, core: 2. Of those that a mesh axis runs over, the one named last changes fastest.
Arguments:
- gate_query: bfloat16 [16384, 512], P(('seq', 'inner'), 'chan'), may hold values from -6 to 6
- gate_key: bfloat16 [16384, 512], P(('seq', 'inner'), 'chan'), may hold values from -6 to 6
- value_input: bfloat16 [16384, 512], P(('seq', 'inner'), 'chan'), may hold values from -6 to 6
- filter_taps: bfloat16 [32, 16384], P('chan', ('seq', 'inner')), may hold values from -4 to 4
- grad_output: bfloat16 [16384, 512], P(('seq', 'inner'), 'chan'), may hold values from -1.5 to 1.5
Outputs:
- mixed_out: bfloat16 [16384, 512], P(('seq', 'inner'), 'chan')
- grad_query: bfloat16 [16384, 512], P(('seq', 'inner'), 'chan')
- grad_key: bfloat16 [16384, 512], P(('seq', 'inner'), 'chan')
- grad_value: bfloat16 [16384, 512], P(('seq', 'inner'), 'chan')
- grad_filter: float32 [32, 16384], P('chan', ('seq', 'inner'))
All inputs are finite; a program needn't handle non-finite values.
Results may differ from a plain program's by a relative error of at most 0.0007.
Values may be sent and summed in bfloat16 or wider, within the bound.
No kernel may reach another device: no remote copies, remote signals or barrier semaphores. Data moves between devices by JAX's collectives and lax.ppermute only.
A program may use at most 64 MiB of HBM per device.

v0:
```python
import math

import jax
import jax.numpy as jnp
from jax import lax
from jax.sharding import PartitionSpec as P

BLOCK = 128


TWO_PI = 2.0 * math.pi
HIGHEST = lax.Precision.HIGHEST


def angles_of(counts, modulus):
    return TWO_PI / modulus * (counts % modulus).astype(jnp.float32)


def rotate(values, angles):
    cosine = jnp.cos(angles)
    sine_part = jnp.sin(angles)
    return jnp.stack(
        (values[0] * cosine - values[1] * sine_part, values[0] * sine_part + values[1] * cosine)
    )


def complex_apply(pattern, matrix, values):
    real_part = jnp.einsum(pattern, matrix[0], values[0], precision=HIGHEST) - jnp.einsum(
        pattern, matrix[1], values[1], precision=HIGHEST
    )
    imag_part = jnp.einsum(pattern, matrix[0], values[1], precision=HIGHEST) + jnp.einsum(
        pattern, matrix[1], values[0], precision=HIGHEST
    )
    return jnp.stack((real_part, imag_part))


def fourier_table(length, orient):
    indices = jnp.arange(length, dtype=jnp.int32)
    angles = orient * angles_of(indices[:, None] * indices[None, :], length)
    return jnp.stack((jnp.cos(angles), jnp.sin(angles)))


def local_forward(values):
    batch_size, seq_len, channels = (values.shape[1], values.shape[2], values.shape[3])
    fold_count = seq_len // BLOCK
    grid_values = values.reshape(2, batch_size, BLOCK, fold_count, channels)
    grid_values = complex_apply("jb,xbaw->xjaw", fourier_table(BLOCK, -1.0), grid_values)
    block_freq = jnp.arange(BLOCK, dtype=jnp.int32)
    fold_index = jnp.arange(fold_count, dtype=jnp.int32)
    grid_values = rotate(
        grid_values, -angles_of(block_freq[:, None] * fold_index[None, :], seq_len)[:, :, None]
    )
    return complex_apply("ca,xjaw->xjcw", fourier_table(fold_count, -1.0), grid_values)


def local_inverse(spectrum):
    batch_size, fold_count, channels = (spectrum.shape[1], spectrum.shape[3], spectrum.shape[4])
    seq_len = BLOCK * fold_count
    grid_values = complex_apply("ac,xjcw->xjaw", fourier_table(fold_count, 1.0), spectrum)
    block_freq = jnp.arange(BLOCK, dtype=jnp.int32)
    fold_index = jnp.arange(fold_count, dtype=jnp.int32)
    grid_values = rotate(
        grid_values, angles_of(block_freq[:, None] * fold_index[None, :], seq_len)[:, :, None]
    )
    grid_values = complex_apply("bj,xjaw->xbaw", fourier_table(BLOCK, 1.0), grid_values)
    return grid_values.reshape(2, batch_size, seq_len, channels)


def back_twists(orders, seq_len, pieces):
    places = jnp.arange(seq_len, dtype=jnp.int32)
    return angles_of(orders[..., None] * places, 2 * seq_len * pieces)


def spread_forward(strided, offset, seq_len):
    pieces, row_count, channels = strided.shape
    outer_count = lax.axis_size("seq")
    inner_count = lax.axis_size("inner")
    halves = jnp.arange(2, dtype=jnp.int32)
    outer_ranks = jnp.arange(outer_count, dtype=jnp.int32)
    inner_ranks = jnp.arange(inner_count, dtype=jnp.int32)
    slow_freq = 2 * outer_ranks[None, :] + halves[:, None]
    first_angles = -angles_of(slow_freq[:, :, None] * outer_ranks[None, None, :], 2 * outer_count)
    grid_in = strided.reshape(outer_count, inner_count, row_count, channels)
    real_part = jnp.einsum("bms,sarw->bmarw", jnp.cos(first_angles), grid_in, precision=HIGHEST)
    imag_part = jnp.einsum("bms,sarw->bmarw", jnp.sin(first_angles), grid_in, precision=HIGHEST)
    turned = -angles_of(slow_freq[:, :, None] * inner_ranks[None, None, :], 2 * pieces)
    sectioned_values = rotate(jnp.stack((real_part, imag_part)), turned[:, :, :, None, None])
    mixed_values = complex_apply(
        "ia,bmarw->bimrw", fourier_table(inner_count, -1.0), sectioned_values
    )
    orders = 2 * jnp.arange(pieces, dtype=jnp.int32)[None, :] + halves[:, None]
    places = offset + jnp.arange(row_count, dtype=jnp.int32)
    twists = -angles_of(orders[:, :, None] * places[None, None, :], 2 * seq_len * pieces)
    return rotate(mixed_values.reshape(2, 2, pieces, row_count, channels), twists[:, :, :, None])


def collect_positions(received, weight):
    pieces, row_count, channels = (received.shape[2], received.shape[3], received.shape[4])
    outer_count = lax.axis_size("seq")
    inner_count = lax.axis_size("inner")
    halves = jnp.arange(2, dtype=jnp.int32)
    outer_ranks = jnp.arange(outer_count, dtype=jnp.int32)
    inner_ranks = jnp.arange(inner_count, dtype=jnp.int32)
    grid_in = received.reshape(2, 2, inner_count, outer_count, row_count, channels)
    sectioned_values = complex_apply("ai,bimrw->bamrw", fourier_table(inner_count, 1.0), grid_in)
    slow_freq = 2 * outer_ranks[None, :] + halves[:, None]
    turned = angles_of(slow_freq[:, None, :] * inner_ranks[None, :, None], 2 * pieces)
    sectioned_values = rotate(sectioned_values, turned[:, :, :, None, None])
    last_angles = angles_of(outer_ranks[:, None, None] * slow_freq[None, :, :], 2 * outer_count)
    result_values = jnp.einsum(
        "sbm,bamrw->sarw", jnp.cos(last_angles) * weight, sectioned_values[0], precision=HIGHEST
    ) - jnp.einsum(
        "sbm,bamrw->sarw", jnp.sin(last_angles) * weight, sectioned_values[1], precision=HIGHEST
    )
    return result_values.reshape(pieces, row_count, channels)


def to_blocks(blocked):
    return lax.all_to_all(blocked, ("seq", "inner"), split_axis=0, concat_axis=0, tiled=True)


def spread_rows(row_term, row_count):
    return lax.psum_scatter(
        row_term(jnp.int32(0), row_count * lax.axis_size(("seq", "inner"))),
        ("seq", "inner"),
        scatter_dimension=0,
        tiled=True,
    )


def forward_blocks(strided, rank_here):
    pieces, row_count, channels = strided.shape
    twisted = spread_forward(strided, rank_here * row_count, pieces * row_count)
    received = lax.all_to_all(twisted, ("seq", "inner"), split_axis=2, concat_axis=2, tiled=True)
    extent = received.shape
    return local_forward(received.reshape(2, 2, extent[2] * extent[3], extent[4]))


def inverse_blocks(spectrum, rank_here, weight):
    values = local_inverse(spectrum)
    seq_len, channels = (values.shape[2], values.shape[3])
    pieces = lax.axis_size(("seq", "inner"))
    row_count = seq_len // pieces
    orders_here = 2 * rank_here + jnp.arange(2, dtype=jnp.int32)
    values = rotate(values, back_twists(orders_here, seq_len, pieces)[..., None])
    blocked = values.reshape(2, 2, pieces, row_count, channels)
    return collect_positions(
        lax.all_to_all(blocked, ("seq", "inner"), split_axis=2, concat_axis=2, tiled=True), weight
    )


def own_filter_spectrum(whole_taps, rank_here, seq_len, pieces):
    group_count = whole_taps.shape[0]
    grid_taps = whole_taps.reshape(group_count, pieces, seq_len)
    orders_here = 2 * rank_here + jnp.arange(2, dtype=jnp.int32)
    ranks_all = jnp.arange(pieces, dtype=jnp.int32)
    angles = -angles_of(orders_here[:, None] * ranks_all[None, :], 2 * pieces)
    real_part = jnp.einsum("bq,gqs->bsg", jnp.cos(angles), grid_taps, precision=HIGHEST)
    imag_part = jnp.einsum("bq,gqs->bsg", jnp.sin(angles), grid_taps, precision=HIGHEST)
    values = rotate(
        jnp.stack((real_part, imag_part)), -back_twists(orders_here, seq_len, pieces)[..., None]
    )
    return local_forward(values)


def multiply_spectra(first, second):
    return jnp.stack(
        (first[0] * second[0] - first[1] * second[1], first[0] * second[1] + first[1] * second[0])
    )


def conjugate_times(first, second):
    return jnp.stack(
        (first[0] * second[0] + first[1] * second[1], first[0] * second[1] - first[1] * second[0])
    )


def per_group(operation, taps_spectrum, spectrum):
    extent = spectrum.shape
    group_count = taps_spectrum.shape[4]
    grouped = spectrum.reshape(extent[:4] + (group_count, extent[4] // group_count))
    return operation(taps_spectrum[..., None], grouped).reshape(extent)


def per_device(gate_query, gate_key, value_input, filter_taps, grad_output):
    pieces = lax.axis_size(("seq", "inner"))
    rank_here = lax.axis_index(("seq", "inner"))
    seq_len, channels = gate_query.shape
    group_count = filter_taps.shape[0]
    row_count = seq_len // pieces
    factor = 1.0 / math.sqrt(seq_len * pieces)
    weight = factor / (2 * seq_len * pieces)
    whole_taps = lax.all_gather(filter_taps, ("seq", "inner"), axis=1, tiled=True).astype(
        jnp.float32
    )
    taps_spectrum = own_filter_spectrum(whole_taps, rank_here, seq_len, pieces)
    query_full = gate_query.astype(jnp.float32)
    key_full = gate_key.astype(jnp.float32)
    value_full = value_input.astype(jnp.float32)
    upstream_full = grad_output.astype(jnp.float32)
    position_product = key_full * value_full
    gated_grad = upstream_full * query_full
    value_spectrum = forward_blocks(
        to_blocks(position_product.reshape(pieces, row_count, channels)), rank_here
    )
    causal = to_blocks(
        inverse_blocks(
            per_group(multiply_spectra, taps_spectrum, value_spectrum), rank_here, weight
        )
    ).reshape(seq_len, channels)
    grad_spectrum = forward_blocks(
        to_blocks(gated_grad.reshape(pieces, row_count, channels)), rank_here
    )
    back_conv = to_blocks(
        inverse_blocks(per_group(conjugate_times, taps_spectrum, grad_spectrum), rank_here, weight)
    ).reshape(seq_len, channels)
    mixed_out = (query_full * causal).astype(jnp.bfloat16)
    grad_query = (upstream_full * causal).astype(jnp.bfloat16)
    grad_key = (back_conv * value_full).astype(jnp.bfloat16)
    grad_value = (back_conv * key_full).astype(jnp.bfloat16)
    cross_full = conjugate_times(value_spectrum, grad_spectrum)
    extent = cross_full.shape
    cross_term = jnp.sum(
        cross_full.reshape(extent[:4] + (group_count, extent[4] // group_count)), axis=5
    )
    orders_here = 2 * rank_here + jnp.arange(2, dtype=jnp.int32)
    taps_values = jnp.transpose(local_inverse(cross_term), (0, 1, 3, 2))
    taps_values = rotate(taps_values, back_twists(orders_here, seq_len, pieces)[:, None, :])

    def filter_rows(block_start, block_total):
        block_rows = jnp.arange(block_total, dtype=jnp.int32)
        phases = angles_of(block_rows[:, None] * orders_here[None, :], 2 * pieces)
        return jnp.einsum(
            "qb,bgs->qgs", jnp.cos(phases) * weight, taps_values[0], precision=HIGHEST
        ) - jnp.einsum("qb,bgs->qgs", jnp.sin(phases) * weight, taps_values[1], precision=HIGHEST)

    grad_filter = spread_rows(filter_rows, 1)[0]
    return (mixed_out, grad_query, grad_key, grad_value, grad_filter)


def solution(mesh):
    placed = (
        P(("seq", "inner"), "chan"),
        P(("seq", "inner"), "chan"),
        P(("seq", "inner"), "chan"),
        P("chan", ("seq", "inner")),
        P(("seq", "inner"), "chan"),
    )
    return jax.shard_map(
        per_device,
        mesh=mesh,
        in_specs=placed,
        out_specs=(
            P(("seq", "inner"), "chan"),
            P(("seq", "inner"), "chan"),
            P(("seq", "inner"), "chan"),
            P(("seq", "inner"), "chan"),
            P("chan", ("seq", "inner")),
        ),
        check_vma=False,
    )
```

profile of v0, /device:TPU:1, one launch (start us, length us, event | category | flops | bytes accessed | tf_op | source)
XLA Modules:
  0.0 1003.6 jit_solution(1493570515501606563)
XLA Ops:
  8.8 16.4 %all-to-all-start.4 = ((f32[128,1,256]{2,1,0:T(1,128)}), f32[128,1,256]{2,1,0:T(1,128)S(1)}, u32[]{:S(2)}, u32[]{:S(2)}) async-start(f32[128,1,256]{2,1,0:T(1,128)} %copy.112), calls=%async_computation.4 | async-start | bytes 262144 | tf_op jit(solution)/shard_map/all_to_all | solution.py:119
  26.0 184.6 %all_gather.3 = bf16[16,16384]{1,0:T(8,128)(2,1)S(1)} all-gather(bf16[16,128]{1,0:T(8,128)(2,1)S(1)} %copy-done.4), channel_id=1, replica_groups=mesh['seq'=16,'inner'=8,'chan'=2] {'seq','inner'}, dimensions={1}, use_global_device_ids=true | all-gather | bytes 528384 | tf_op jit(solution)/shard_map/all_gather | solution.py:193
  212.1 5.9 all-to-all-start
  219.1 12.9 %all-to-all-done = f32[128,1,256]{2,1,0:T(1,128)S(1)} async-done(((f32[128,1,256]{2,1,0:T(1,128)}), f32[128,1,256]{2,1,0:T(1,128)S(1)}, u32[]{:S(2)}, u32[]{:S(2)}) %all-to-all-start) | async-done | bytes 131104 | tf_op jit(solution)/shard_map/all_to_all | solution.py:119
  237.8 1.2 copy.121
  239.0 5.6 all-to-all-start.5
  246.9 1.2 copy.98
  248.2 18.6 %all-to-all-done.5 = f32[2,2,128,1,256]{4,1,3,0,2:T(2,128)S(1)} async-done(((f32[2,2,128,1,256]{4,1,3,0,2:T(2,128)}), f32[2,2,128,1,256]{4,1,3,0,2:T(2,128)S(1)}, u32[]{:S(2)}, u32[]{:S(2)}) %all-to-all-start.5) | async-done | bytes 524320 | tf_op jit(solution)/shard_map/all_to_all | solution.py:134
  266.8 5.7 all-to-all-start.1
  275.0 19.5 %all-to-all-done.1 = f32[2,2,128,1,256]{4,1,3,0,2:T(2,128)S(1)} async-done(((f32[2,2,128,1,256]{4,1,3,0,2:T(2,128)}), f32[2,2,128,1,256]{4,1,3,0,2:T(2,128)S(1)}, u32[]{:S(2)}, u32[]{:S(2)}) %all-to-all-start.1) | async-done | bytes 524320 | tf_op jit(solution)/shard_map/all_to_all | solution.py:134
  303.6 1.0 copy.124
  304.6 5.7 all-to-all-start.6
  310.4 1.0 copy.101
  313.4 1.1 fusion.146
  314.5 18.0 %all-to-all-done.6 = f32[2,2,128,1,256]{4,1,0,3,2:T(2,128)S(1)} async-done(((f32[2,2,128,1,256]{4,1,0,3,2:T(2,128)}), f32[2,2,128,1,256]{4,1,0,3,2:T(2,128)S(1)}, u32[]{:S(2)}, u32[]{:S(2)}) %all-to-all-start.6) | async-done | bytes 524320 | tf_op jit(solution)/shard_map/all_to_all | solution.py:148
  332.5 5.5 all-to-all-start.2
  338.0 1.2 convolution_subtract_fusion
  339.2 1.6 copy.137
  342.6 17.5 %all-to-all-done.2 = f32[2,2,128,1,256]{4,1,0,3,2:T(2,128)S(1)} async-done(((f32[2,2,128,1,256]{4,1,0,3,2:T(2,128)}), f32[2,2,128,1,256]{4,1,0,3,2:T(2,128)S(1)}, u32[]{:S(2)}, u32[]{:S(2)}) %all-to-all-start.2) | async-done | bytes 524320 | tf_op jit(solution)/shard_map/all_to_all | solution.py:148
  364.8 5.4 all-to-all-start.3
  371.9 12.4 %all-to-all-done.3 = f32[128,1,256]{2,1,0:T(1,128)S(1)} async-done(((f32[128,1,256]{2,1,0:T(1,128)}), f32[128,1,256]{2,1,0:T(1,128)S(1)}, u32[]{:S(2)}, u32[]{:S(2)}) %all-to-all-start.3) | async-done | bytes 131104 | tf_op jit(solution)/shard_map/all_to_all | solution.py:119
  384.3 5.6 all-to-all-start.7
  390.5 13.3 %all-to-all-done.7 = f32[128,1,256]{2,1,0:T(1,128)S(1)} async-done(((f32[128,1,256]{2,1,0:T(1,128)}), f32[128,1,256]{2,1,0:T(1,128)S(1)}, u32[]{:S(2)}, u32[]{:S(2)}) %all-to-all-start.7) | async-done | bytes 131104 | tf_op jit(solution)/shard_map/all_to_all | solution.py:119
  404.6 591.9 %reduce-scatter.2.cloned.1.call-done = f32[1,16,128]{2,1,0:T(8,128)} async-done(((f32[128,16,128]{2,1,0:T(8,128)}), f32[1,16,128]{2,1,0:T(8,128)}) %reduce-scatter.2.cloned.1.call-update) | async-done | bytes 8208 | tf_op jit(solution)/shard_map/reduce_scatter | solution.py:123
  (110 shorter events, 35.7 us)
Async XLA Ops:
  8.8 203.3 %all-to-all-start.4 = ((f32[128,1,256]{2,1,0:T(1,128)}), f32[128,1,256]{2,1,0:T(1,128)S(1)}, u32[]{:S(2)}, u32[]{:S(2)}) async-start(f32[128,1,256]{2,1,0:T(1,128)} %copy.112), calls=%async_computation.4 | async-start | bytes 262144 | tf_op jit(solution)/shard_map/all_to_all | solution.py:119
  25.4 0.7 copy-start.4
  26.0 184.7 %copy-start.2 = (bf16[128,256]{1,0:T(8,128)(2,1)S(1)}, bf16[128,256]{1,0:T(8,128)(2,1)}, u32[]{:S(2)}) copy-start(bf16[128,256]{1,0:T(8,128)(2,1)} %param.7) | copy-start | bytes 196612
  26.0 184.8 %copy-start.3 = (bf16[128,256]{1,0:T(8,128)(2,1)S(1)}, bf16[128,256]{1,0:T(8,128)(2,1)}, u32[]{:S(2)}) copy-start(bf16[128,256]{1,0:T(8,128)(2,1)} %param.6) | copy-start | bytes 196612
  212.1 19.8 %all-to-all-start = ((f32[128,1,256]{2,1,0:T(1,128)}), f32[128,1,256]{2,1,0:T(1,128)S(1)}, u32[]{:S(2)}, u32[]{:S(2)}) async-start(f32[128,1,256]{2,1,0:T(1,128)} %reshape.1125), calls=%async_computation | async-start | bytes 262144 | tf_op jit(solution)/shard_map/all_to_all | solution.py:119
  239.0 27.7 %all-to-all-start.5 = ((f32[2,2,128,1,256]{4,1,3,0,2:T(2,128)}), f32[2,2,128,1,256]{4,1,3,0,2:T(2,128)S(1)}, u32[]{:S(2)}, u32[]{:S(2)}) async-start(f32[2,2,128,1,256]{4,1,3,0,2:T(2,128)} %copy.121), calls=%async_computation.5 | async-start | bytes 1048576 | tf_op jit(solution)/shard_map/all_to_all | solution.py:134
  266.8 27.8 %all-to-all-start.1 = ((f32[2,2,128,1,256]{4,1,3,0,2:T(2,128)}), f32[2,2,128,1,256]{4,1,3,0,2:T(2,128)S(1)}, u32[]{:S(2)}, u32[]{:S(2)}) async-start(f32[2,2,128,1,256]{4,1,3,0,2:T(2,128)} %copy.98), calls=%async_computation.1 | async-start | bytes 1048576 | tf_op jit(solution)/shard_map/all_to_all | solution.py:134
  304.6 27.8 %all-to-all-start.6 = ((f32[2,2,128,1,256]{4,1,0,3,2:T(2,128)}), f32[2,2,128,1,256]{4,1,0,3,2:T(2,128)S(1)}, u32[]{:S(2)}, u32[]{:S(2)}) async-start(f32[2,2,128,1,256]{4,1,0,3,2:T(2,128)} %copy.124), calls=%async_computation.6 | async-start | bytes 1048576 | tf_op jit(solution)/shard_map/all_to_all | solution.py:148
  332.5 27.6 %all-to-all-start.2 = ((f32[2,2,128,1,256]{4,1,0,3,2:T(2,128)}), f32[2,2,128,1,256]{4,1,0,3,2:T(2,128)S(1)}, u32[]{:S(2)}, u32[]{:S(2)}) async-start(f32[2,2,128,1,256]{4,1,0,3,2:T(2,128)} %copy.101), calls=%async_computation.2 | async-start | bytes 1048576 | tf_op jit(solution)/shard_map/all_to_all | solution.py:148
  338.0 658.5 %reduce-scatter.2.cloned.1.call-start = ((), (), s32[]{:S(2)}) async-start(), calls=%async_computation.9 | async-start | bytes 1056768 | tf_op jit(solution)/shard_map/reduce_scatter | solution.py:123
  364.8 19.5 %all-to-all-start.3 = ((f32[128,1,256]{2,1,0:T(1,128)}), f32[128,1,256]{2,1,0:T(1,128)S(1)}, u32[]{:S(2)}, u32[]{:S(2)}) async-start(f32[128,1,256]{2,1,0:T(1,128)} %copy.111), calls=%async_computation.3 | async-start | bytes 262144 | tf_op jit(solution)/shard_map/all_to_all | solution.py:119
  371.9 17.9 %copy-start = (bf16[128,256]{1,0:T(8,128)(2,1)S(1)}, bf16[128,256]{1,0:T(8,128)(2,1)}, u32[]{:S(2)}) copy-start(bf16[128,256]{1,0:T(8,128)(2,1)} %param.9) | copy-start | bytes 196612
  371.9 18.0 %copy-start.1 = (bf16[128,256]{1,0:T(8,128)(2,1)S(1)}, bf16[128,256]{1,0:T(8,128)(2,1)}, u32[]{:S(2)}) copy-start(bf16[128,256]{1,0:T(8,128)(2,1)} %param.5) | copy-start | bytes 196612
  384.3 19.6 %all-to-all-start.7 = ((f32[128,1,256]{2,1,0:T(1,128)}), f32[128,1,256]{2,1,0:T(1,128)S(1)}, u32[]{:S(2)}, u32[]{:S(2)}) async-start(f32[128,1,256]{2,1,0:T(1,128)} %copy.134), calls=%async_computation.7 | async-start | bytes 262144 | tf_op jit(solution)/shard_map/all_to_all | solution.py:119
Sparse Core Ops, SparseCore 0:
  341.9 654.5 reduce-scatter.1
where the time goes:
time: 1020 us; the launch traced here: 1000 us
  waiting for transfers between devices  704 us (69%)
  blocking collectives  185 us (18%)
  starting transfers between devices  55.8 us (5%)
  matrix products  28.8 us (3%)
  between operations  15 us (1%)
  local copies, waits for them, and re-layouts  11.7 us (1%)
    reduce_scatter x1, waiting for transfers between devices, spread_rows(): lax.psum_scatter(row_term(jnp.int32(0), row_count * lax.axis_size(('seq',...  592 us
    all_gather x1, blocking collectives, per_device(): lax.all_gather(filter_taps, ('seq', 'inner'), axis=1, tiled=True)  185 us
    all_to_all x4, waiting for transfers between devices, to_blocks(): lax.all_to_all(blocked, ('seq', 'inner'), split_axis=0, concat_axis=0, ti...  38.6 us
    all_to_all x2, waiting for transfers between devices, forward_blocks(): lax.all_to_all(twisted, ('seq', 'inner'), split_axis=2, concat_axis=2, ti...  38.2 us
    all_to_all x2, waiting for transfers between devices, inverse_blocks(): lax.all_to_all(blocked, ('seq', 'inner'), split_axis=2, concat_axis=2, ti...  35.5 us
    all_to_all x4, starting transfers between devices, to_blocks(): lax.all_to_all(blocked, ('seq', 'inner'), split_axis=0, concat_axis=0, ti...  33.3 us
  transfers between devices with their start and end apart: 9, of which 8 were waited for; matrix products, arithmetic and copies ran while one was open for 2% of the time, Pallas kernels for 0%

commit v1 on v0

v1 whole, which is shorter than its diff:
```python
import math

import jax
import jax.numpy as jnp
import numpy as np
from jax import lax
from jax.experimental import pallas as pl
from jax.experimental.pallas import tpu as pltpu
from jax.sharding import PartitionSpec as P

AXES = ("seq", "inner")
PIECES = 128
ROWS = 128
CHANNELS = 256
GROUPS = 16
LENGTH = PIECES * ROWS
PADDED = 2 * LENGTH
OUTER = 2 * PIECES
SLOTS = 5
F32 = jnp.float32
BF16 = jnp.bfloat16


def split_table(table):
    high = table.astype(np.float32).astype(jnp.bfloat16)
    low = (table - high.astype(np.float64)).astype(jnp.bfloat16)
    return high, low


def tables():
    k1 = np.arange(OUTER)
    t1 = np.arange(PIECES)
    t2 = np.arange(ROWS)
    outer = np.exp(-2j * np.pi * ((k1[:, None] * t1[None, :]) % OUTER) / OUTER)
    inner = np.exp(-2j * np.pi * ((t2[:, None] * t2[None, :]) % ROWS) / ROWS)
    twist = np.exp(-2j * np.pi * (k1[:, None] * t2[None, :]) / PADDED)
    first = np.concatenate((outer.real, outer.imag), axis=0)
    second = np.block([[inner.real, inner.imag], [-inner.imag, inner.real]])
    scale = 1.0 / (math.sqrt(LENGTH) * PADDED)
    last = np.concatenate((outer.real.T, outer.imag.T), axis=0) * scale
    first_high, first_low = split_table(first)
    second_high, second_low = split_table(second)
    last_high, last_low = split_table(last)
    return (
        np.concatenate((first_high, first_low, first_high), axis=1),
        np.concatenate((second_high, second_high, second_low), axis=0),
        np.stack((twist.real, twist.imag)).astype(np.float32),
        np.concatenate((last_high, last_high, last_low), axis=1),
    )


def split(values):
    high = values.astype(BF16)
    low = (values - high.astype(F32)).astype(BF16)
    return high, low


def dot(left, right):
    return jnp.dot(left, right, preferred_element_type=F32)


def slot(ref, index):
    return ref[pl.ds(index, PIECES, stride=SLOTS), :]


def put_slot(ref, index, values):
    ref[pl.ds(index, PIECES, stride=SLOTS), :] = values


def pack_kernel(query_ref, key_ref, value_ref, taps_ref, upstream_ref, out_ref):
    def place(first, left, right):
        product = left[...].astype(F32) * right[...].astype(F32)
        turned = jnp.transpose(product).reshape(GROUPS, 2, 8, ROWS)
        put_slot(out_ref, first, turned[:, 0].reshape(PIECES, ROWS))
        put_slot(out_ref, first + 1, turned[:, 1].reshape(PIECES, ROWS))

    place(0, key_ref, value_ref)
    place(2, upstream_ref, query_ref)
    taps = taps_ref[...].astype(F32)
    spread = jnp.broadcast_to(taps[:, None, :], (GROUPS, 8, ROWS)).reshape(PIECES, ROWS)
    put_slot(out_ref, 4, spread)


def convolve_kernel(in_ref, first_ref, second_ref, twist_ref, last_ref, out_ref):
    whole = jnp.concatenate([slot(in_ref, i) for i in range(SLOTS)], axis=1)
    high, low = split(whole)
    mixed = dot(first_ref[...], jnp.concatenate((high, high, low), axis=0))
    twist_real, twist_imag = twist_ref[0], twist_ref[1]

    def part(half, index):
        return mixed[half * OUTER : (half + 1) * OUTER, index * ROWS : (index + 1) * ROWS]

    def rotate(real, imag, sign):
        return (
            real * twist_real - sign * (imag * twist_imag),
            imag * twist_real + sign * (real * twist_imag),
        )

    def pair(index):
        return (
            part(0, index) - part(1, index + 1),
            part(1, index) + part(0, index + 1),
        )

    def inner(real, imag):
        high, low = split(jnp.concatenate((real, imag), axis=1))
        result = dot(jnp.concatenate((high, low, high), axis=1), second_ref[...])
        return result[:, :ROWS], result[:, ROWS:]

    value_real, value_imag = inner(*rotate(*pair(0), 1.0))
    grad_real, grad_imag = inner(*rotate(*pair(2), 1.0))
    taps_real, taps_imag = inner(*rotate(part(0, 4), part(1, 4), 1.0))

    def back(real, imag):
        turned_imag, turned_real = inner(imag, real)
        return jnp.concatenate(rotate(turned_real, turned_imag, -1.0), axis=1)

    spectra = jnp.concatenate(
        (
            back(
                value_real * taps_real - value_imag * taps_imag,
                value_real * taps_imag + value_imag * taps_real,
            ),
            back(
                grad_real * taps_real + grad_imag * taps_imag,
                grad_imag * taps_real - grad_real * taps_imag,
            ),
            back(
                grad_real * value_real + grad_imag * value_imag,
                grad_imag * value_real - grad_real * value_imag,
            ),
        ),
        axis=1,
    )
    high, low = split(spectra)
    final = dot(last_ref[...], jnp.concatenate((high, low, high), axis=0))

    def block(half, index):
        return final[half * PIECES : (half + 1) * PIECES, index * ROWS : (index + 1) * ROWS]

    put_slot(out_ref, 0, block(0, 0) + block(1, 1))
    put_slot(out_ref, 1, block(0, 1) - block(1, 0))
    put_slot(out_ref, 2, block(0, 2) + block(1, 3))
    put_slot(out_ref, 3, block(0, 3) - block(1, 2))
    put_slot(out_ref, 4, block(0, 4) + block(1, 5))


def finish_kernel(
    in_ref, query_ref, key_ref, value_ref, upstream_ref, mixed_ref, gquery_ref, gkey_ref, gvalue_ref, gfilter_ref
):
    def collect(first):
        one = slot(in_ref, first).reshape(GROUPS, 1, 8, ROWS)
        two = slot(in_ref, first + 1).reshape(GROUPS, 1, 8, ROWS)
        return jnp.transpose(jnp.concatenate((one, two), axis=1).reshape(CHANNELS, ROWS))

    causal = collect(0)
    mixed_ref[...] = (query_ref[...].astype(F32) * causal).astype(BF16)
    gquery_ref[...] = (upstream_ref[...].astype(F32) * causal).astype(BF16)
    back_conv = collect(2)
    gkey_ref[...] = (back_conv * value_ref[...].astype(F32)).astype(BF16)
    gvalue_ref[...] = (back_conv * key_ref[...].astype(F32)).astype(BF16)
    gfilter_ref[...] = jnp.sum(slot(in_ref, 4).reshape(GROUPS, 8, ROWS), axis=1)


def exchange(blocks):
    return lax.all_to_all(
        blocks.reshape(PIECES * SLOTS, 1, ROWS), AXES, split_axis=0, concat_axis=0, tiled=True
    ).reshape(PIECES * SLOTS, ROWS)


def per_device(gate_query, gate_key, value_input, filter_taps, grad_output):
    packed = jax.ShapeDtypeStruct((PIECES * SLOTS, ROWS), F32)
    blocks = pl.pallas_call(pack_kernel, out_shape=packed)(
        gate_query, gate_key, value_input, filter_taps, grad_output
    )
    received = exchange(blocks)
    results = pl.pallas_call(
        convolve_kernel,
        out_shape=packed,
        compiler_params=pltpu.CompilerParams(vmem_limit_bytes=48 * 1024 * 1024),
    )(received, *(jnp.asarray(table) for table in tables()))
    returned = exchange(results)
    wide = jax.ShapeDtypeStruct((ROWS, CHANNELS), BF16)
    return pl.pallas_call(
        finish_kernel,
        out_shape=(wide, wide, wide, wide, jax.ShapeDtypeStruct((GROUPS, ROWS), F32)),
    )(returned, gate_query, gate_key, value_input, grad_output)


def solution(mesh):
    rows = P(AXES, "chan")
    taps = P("chan", AXES)
    return jax.shard_map(
        per_device,
        mesh=mesh,
        in_specs=(rows, rows, rows, taps, rows),
        out_specs=(rows, rows, rows, rows, taps),
        check_vma=False,
    )
```

time: 1020 us -> 65.5 us (0.06); the launches traced: 1000 us -> 65.2 us
  waiting for transfers between devices: 704 us -> 0 us
  blocking collectives: 185 us -> 58.1 us
  starting transfers between devices: 55.8 us -> 0 us
  matrix products: 28.8 us -> 0 us
  between operations: 15 us -> 0.67 us
  local copies, waits for them, and re-layouts: 11.7 us -> 0.96 us
    reduce_scatter x1 -> x0, waiting for transfers between devices: 592 us -> none  [spread_rows(): lax.psum_scatter(row_term(jnp.int32(0), row_count * lax.axis_size(('seq',...]
    all_gather x1 -> x0, blocking collectives: 185 us -> none  [per_device(): lax.all_gather(filter_taps, ('seq', 'inner'), axis=1, tiled=True)]
    all_to_all x8 -> x0, waiting for transfers between devices: 112 us -> none  [the longest x4 38.6 us: to_blocks(): lax.all_to_all(blocked, ('seq', 'inner'), split_axis=0, concat_axis=0, ti...]
    all_to_all x0 -> x2, blocking collectives: none -> 58.1 us  [exchange(): lax.all_to_all(blocks.reshape(PIECES * SLOTS, 1, ROWS), AXES, split_axis=...]
    all_to_all x8 -> x0, starting transfers between devices: 55.8 us -> none  [the longest x4 33.3 us: to_blocks(): lax.all_to_all(blocked, ('seq', 'inner'), split_axis=0, concat_axis=0, ti...]
    dot_general x52 -> x0, matrix products: 28.8 us -> none  [the longest x10 5.7 us: complex_apply(): jnp.einsum(pattern, matrix[1], values[1], precision=HIGHEST)]
  transfers between devices with their start and end apart: 9 -> 0, of which waited for: 8 -> 0; matrix products, arithmetic and copies ran while one was open for 2% -> 0% of each run, Pallas kernels for 0% -> 0%
where the time goes in v1:
time: 65.5 us; the launch traced here: 65.2 us
  blocking collectives  58.1 us (89%)
  Pallas kernels  5.5 us (8%)
  local copies, waits for them, and re-layouts  0.96 us (1%)
  between operations  0.67 us (1%)
    all_to_all x2, blocking collectives, exchange(): lax.all_to_all(blocks.reshape(PIECES * SLOTS, 1, ROWS), AXES, split_axis=...  58.1 us
    pallas_call x1, Pallas kernels, per_device(): pl.pallas_call(pack_kernel, out_shape=packed)  1.88 us
    pallas_call x1, Pallas kernels, per_device(): pl.pallas_call(finish_kernel, out_shape=(wide, wide, wide, wide, jax.Shap...  1.85 us
    pallas_call x1, Pallas kernels, per_device(): pl.pallas_call(convolve_kernel, out_shape=packed, compiler_params=pltpu.C...  1.77 us

profile of v1, /device:TPU:1, one launch (start us, length us, event | category | flops | bytes accessed | tf_op | source)
XLA Modules:
  0.0 65.2 jit_solution(9769236546586557921)
XLA Ops:
  0.6 0.0 copy-start.1
  0.6 0.0 copy-start.2
  0.7 1.9 %shard_map.128 = f32[640,128]{1,0:T(8,128)} custom-call(bf16[128,256]{1,0:T(8,128)(2,1)} %query_ref.3, bf16[128,256]{1,0:T(8,128)(2,1)} %key_ref.3, bf16[128,256]{1,0:T(8,128)(2,1)} %value_ref.3, bf16[16,128]{1,0:T(8,128)(2,1)} %taps_ref.1, bf16[128,256]{1,0:T(8,128)(2,1)} %upstream_ref.3), custom_call_target="tpu_custom_call" | custom-call | tf_op jit(solution)/shard_map/pallas_call | solution.py:173
  2.5 0.0 copy-start
  2.5 34.5 %all_to_all.10 = f32[640,1,128]{2,1,0:T(1,128)S(1)} all-to-all(f32[640,1,128]{2,1,0:T(1,128)} %bitcast.11), channel_id=1, replica_groups=mesh['seq'=16,'inner'=8,'chan'=2] {'seq','inner'}, dimensions={0} | all-to-all | bytes 655360 | tf_op jit(solution)/shard_map/all_to_all | solution.py:166
  37.0 0.0 copy-done.1
  37.0 0.0 copy-done.2
  37.0 0.0 copy-done
  37.0 0.0 copy-start.3
  37.0 0.9 %copy-done.3 = f32[2,256,128]{2,1,0:T(8,128)S(1)} copy-done((f32[2,256,128]{2,1,0:T(8,128)S(1)}, f32[2,256,128]{2,1,0:T(8,128)}, u32[]{:S(2)}) %copy-start.3) | copy-done | bytes 262168
  38.0 1.8 %shard_map.129 = f32[640,128]{1,0:T(8,128)S(1)} custom-call(f32[640,128]{1,0:T(8,128)S(1)} %bitcast.8, bf16[512,384]{1,0:T(8,128)(2,1)S(1)} %copy-done.2, bf16[768,256]{1,0:T(8,128)(2,1)S(1)} %copy-done.1, f32[2,256,128]{2,1,0:T(8,128)S(1)} %copy-done.3, bf16[256,768]{1,0:T(8,128)(2,1)S(1)} %copy-done), custom_call_target="tpu_custom_call" | custom-call | tf_op jit(solution)/shard_map/pallas_call | solution.py:177
  39.7 23.6 %all_to_all.11 = f32[640,1,128]{2,1,0:T(1,128)} all-to-all(f32[640,1,128]{2,1,0:T(1,128)S(1)} %bitcast.9), channel_id=1, replica_groups=mesh['seq'=16,'inner'=8,'chan'=2] {'seq','inner'}, dimensions={0} | all-to-all | bytes 655360 | tf_op jit(solution)/shard_map/all_to_all | solution.py:166
  63.4 1.9 %shard_map.130 = (bf16[128,256]{1,0:T(8,128)(2,1)}, bf16[128,256]{1,0:T(8,128)(2,1)}, bf16[128,256]{1,0:T(8,128)(2,1)}, bf16[128,256]{1,0:T(8,128)(2,1)}, f32[16,128]{1,0:T(8,128)}) custom-call(f32[640,128]{1,0:T(8,128)} %bitcast.10, bf16[128,256]{1,0:T(8,128)(2,1)} %query_ref.3, bf16[128,256]{1,0:T(8,128)(2,1)} %key_ref.3, bf16[128,256]{1,0:T(8,128)(2,1)} %value_ref.3, ...), custom_call_target="tpu_custom_call" | custom-call | tf_op jit(solution)/shard_map/pallas_call | solution.py:184
Async XLA Ops:
  0.6 36.4 %copy-start.1 = (bf16[768,256]{1,0:T(8,128)(2,1)S(1)}, bf16[768,256]{1,0:T(8,128)(2,1)}, u32[]{:S(2)}) copy-start(bf16[768,256]{1,0:T(8,128)(2,1)} %constant.9.clone.second_ref) | copy-start | bytes 1179652
  0.6 36.4 %copy-start.2 = (bf16[512,384]{1,0:T(8,128)(2,1)S(1)}, bf16[512,384]{1,0:T(8,128)(2,1)}, u32[]{:S(2)}) copy-start(bf16[512,384]{1,0:T(8,128)(2,1)} %constant.8.clone.first_ref) | copy-start | bytes 1179652
  2.5 34.5 %copy-start = (bf16[256,768]{1,0:T(8,128)(2,1)S(1)}, bf16[256,768]{1,0:T(8,128)(2,1)}, u32[]{:S(2)}) copy-start(bf16[256,768]{1,0:T(8,128)(2,1)} %constant.11.clone.last_ref) | copy-start | bytes 1179652
  37.0 1.0 %copy-start.3 = (f32[2,256,128]{2,1,0:T(8,128)S(1)}, f32[2,256,128]{2,1,0:T(8,128)}, u32[]{:S(2)}) copy-start(f32[2,256,128]{2,1,0:T(8,128)} %constant.10.clone.twist_ref) | copy-start | bytes 786436

commit v2 on v1

v2 whole, which is shorter than its diff:
```python
import math

import jax
import jax.numpy as jnp
import numpy as np
from jax import lax
from jax.experimental import pallas as pl
from jax.experimental.pallas import tpu as pltpu
from jax.sharding import PartitionSpec as P

AXES = ("seq", "inner")
PIECES = 128
CHIPS = PIECES // 2
ROWS = 128
CHANNELS = 256
GROUPS = 16
SUBS = CHIPS // GROUPS
OWNED = 4
LENGTH = PIECES * ROWS
PADDED = 2 * LENGTH
OUTER = 2 * PIECES
SLOTS = 2 * OWNED + 1
SMALL = 4 * 1024 * 1024
LARGE = 24 * 1024 * 1024
F32 = jnp.float32
BF16 = jnp.bfloat16


def split_table(table):
    high = table.astype(np.float32).astype(jnp.bfloat16)
    low = (table - high.astype(np.float64)).astype(jnp.bfloat16)
    return high, low


def tables():
    k1 = np.arange(OUTER)
    t1 = np.stack((np.arange(0, PIECES, 2), np.arange(1, PIECES, 2)))
    t2 = np.arange(ROWS)
    outer = np.exp(-2j * np.pi * ((k1[None, :, None] * t1[:, None, :]) % OUTER) / OUTER)
    inner = np.exp(-2j * np.pi * ((t2[:, None] * t2[None, :]) % ROWS) / ROWS)
    twist = np.exp(-2j * np.pi * (k1[:, None] * t2[None, :]) / PADDED)
    first = np.concatenate((outer.real, outer.imag), axis=1)
    second = np.block([[inner.real, inner.imag], [-inner.imag, inner.real]])
    scale = 1.0 / (math.sqrt(LENGTH) * PADDED)
    last = np.swapaxes(np.concatenate((outer.real, outer.imag), axis=2), 1, 2) * scale
    first_high, first_low = split_table(first)
    second_high, second_low = split_table(second)
    last_high, last_low = split_table(last)
    return (
        np.concatenate((first_high, first_low, first_high), axis=2),
        np.concatenate((second_high, second_low), axis=0),
        np.stack((twist.real, twist.imag)).astype(np.float32),
        np.concatenate((last_high, last_low), axis=2),
    )


def split(values):
    high = values.astype(BF16)
    low = (values - high.astype(F32)).astype(BF16)
    return high, low


def dot(left, right):
    return jnp.dot(left, right, preferred_element_type=F32)


def chip_rows(slot, first=0, count=CHIPS, slots=SLOTS):
    return pl.ds(first * slots + slot, count, stride=slots)


def slot_of(array, owned):
    return 4 * (owned // 2) + 2 * array + owned % 2


def pack_kernel(
    query_ref, key_ref, value_ref, taps_ref, upstream_ref, out_ref, query, key, value, taps, upstream, turned, sems
):
    moves = (
        (key_ref, key),
        (value_ref, value),
        (upstream_ref, upstream),
        (query_ref, query),
        (taps_ref, taps),
    )
    copies = [pltpu.make_async_copy(a, b, sems.at[i]) for i, (a, b) in enumerate(moves)]
    for copy in copies:
        copy.start()

    def place(array, left, right):
        turned[array] = jnp.transpose(left[...].astype(F32) * right[...].astype(F32))
        for owned in range(OWNED):
            for sub in range(SUBS):
                out_ref[chip_rows(slot_of(array, owned), GROUPS * sub, GROUPS), :] = turned[
                    array, pl.ds(SUBS * owned + sub, GROUPS, stride=GROUPS), :
                ]

    copies[0].wait()
    copies[1].wait()
    place(0, key, value)
    copies[2].wait()
    copies[3].wait()
    place(1, upstream, query)
    copies[4].wait()
    for sub in range(SUBS):
        out_ref[chip_rows(SLOTS - 1, GROUPS * sub, GROUPS), :] = taps[...].astype(F32)


def outer_forward(in_ref, table):
    whole = jnp.concatenate([in_ref[chip_rows(i), :] for i in range(SLOTS)], axis=1)
    high, low = split(whole)
    return dot(table, jnp.concatenate((high, high, low), axis=0))


def own_kernel(core_ref, in_ref, first_ref, out_ref):
    out_ref[...] = outer_forward(in_ref, first_ref[core_ref[0]])


def convolve_kernel(core_ref, other_ref, mixed_ref, first_ref, second_ref, twist_ref, last_ref, out_ref):
    core = core_ref[0]
    mixed = mixed_ref[...] + outer_forward(other_ref, first_ref[1 - core])
    second = jnp.concatenate(
        (second_ref[: 2 * ROWS], second_ref[: 2 * ROWS], second_ref[2 * ROWS :]), axis=0
    )
    twist_real, twist_imag = twist_ref[0], twist_ref[1]

    def part(half, index):
        return mixed[half * OUTER : (half + 1) * OUTER, index * ROWS : (index + 1) * ROWS]

    def rotate(real, imag, sign):
        return (
            real * twist_real - sign * (imag * twist_imag),
            imag * twist_real + sign * (real * twist_imag),
        )

    def inner(real, imag):
        high, low = split(jnp.concatenate((real, imag), axis=1))
        result = dot(jnp.concatenate((high, low, high), axis=1), second)
        return result[:, :ROWS], result[:, ROWS:]

    def forward(slot):
        return inner(
            *rotate(part(0, slot) - part(1, slot + 1), part(1, slot) + part(0, slot + 1), 1.0)
        )

    def back(real, imag):
        turned_imag, turned_real = inner(imag, real)
        return jnp.concatenate(rotate(turned_real, turned_imag, -1.0), axis=1)

    taps_real, taps_imag = inner(*rotate(part(0, SLOTS - 1), part(1, SLOTS - 1), 1.0))
    spectra = []
    cross_real = cross_imag = None
    for pair in range(2):
        value_real, value_imag = forward(4 * pair)
        spectra.append(
            back(
                value_real * taps_real - value_imag * taps_imag,
                value_real * taps_imag + value_imag * taps_real,
            )
        )
        grad_real, grad_imag = forward(4 * pair + 2)
        spectra.append(
            back(
                grad_real * taps_real + grad_imag * taps_imag,
                grad_imag * taps_real - grad_real * taps_imag,
            )
        )
        term_real = grad_real * value_real + grad_imag * value_imag
        term_imag = grad_imag * value_real - grad_real * value_imag
        cross_real = term_real if cross_real is None else cross_real + term_real
        cross_imag = term_imag if cross_imag is None else cross_imag + term_imag
    spectra.append(back(cross_real, cross_imag))
    high, low = split(jnp.concatenate(spectra, axis=1))
    table = last_ref[core]
    last = jnp.concatenate((table[:, :OUTER], table[:, :OUTER], table[:, OUTER:]), axis=1)
    final = dot(last, jnp.concatenate((high, low, high), axis=0))

    def block(half, index):
        return final[half * CHIPS : (half + 1) * CHIPS, index * ROWS : (index + 1) * ROWS]

    for index in range(0, 2 * OWNED, 2):
        out_ref[chip_rows(index), :] = block(0, index) + block(1, index + 1)
        out_ref[chip_rows(index + 1), :] = block(0, index + 1) - block(1, index)
    out_ref[chip_rows(SLOTS - 1), :] = block(0, SLOTS - 1) + block(1, SLOTS)


def finish_kernel(
    in_ref, query_ref, key_ref, value_ref, upstream_ref, mixed_ref, gquery_ref, gkey_ref, gvalue_ref, gfilter_ref, turned
):
    def collect(array):
        for owned in range(OWNED):
            for sub in range(SUBS):
                turned[array, pl.ds(SUBS * owned + sub, GROUPS, stride=GROUPS), :] = in_ref[
                    chip_rows(slot_of(array, owned), GROUPS * sub, GROUPS), :
                ]
        return jnp.transpose(turned[array])

    causal = collect(0)
    mixed_ref[...] = (query_ref[...].astype(F32) * causal).astype(BF16)
    gquery_ref[...] = (upstream_ref[...].astype(F32) * causal).astype(BF16)
    back_conv = collect(1)
    gkey_ref[...] = (back_conv * value_ref[...].astype(F32)).astype(BF16)
    gvalue_ref[...] = (back_conv * key_ref[...].astype(F32)).astype(BF16)
    parts = [in_ref[chip_rows(SLOTS - 1, GROUPS * sub, GROUPS), :] for sub in range(SUBS)]
    gfilter_ref[...] = (parts[0] + parts[1]) + (parts[2] + parts[3])


def swap_cores(values):
    count = lax.axis_size("inner")
    return lax.ppermute(values, "inner", [(i, i ^ 1) for i in range(count)])


def exchange(blocks):
    groups = [list(range(core, PIECES, 2)) for core in range(2)]
    return lax.all_to_all(
        blocks.reshape(CHIPS * SLOTS, 1, ROWS),
        AXES,
        split_axis=0,
        concat_axis=0,
        tiled=True,
        axis_index_groups=groups,
    ).reshape(CHIPS * SLOTS, ROWS)


def per_device(gate_query, gate_key, value_input, filter_taps, grad_output):
    core = (lax.axis_index("inner") % 2).astype(jnp.int32).reshape(1)
    scalar = pl.BlockSpec(memory_space=pltpu.SMEM)
    whole = pl.BlockSpec(memory_space=pltpu.VMEM)
    small = pltpu.CompilerParams(vmem_limit_bytes=SMALL)
    packed = jax.ShapeDtypeStruct((CHIPS * SLOTS, ROWS), F32)
    turned = pltpu.VMEM((2, CHANNELS, ROWS), F32)
    far = pl.BlockSpec(memory_space=pltpu.HBM)
    wide = pltpu.VMEM((ROWS, CHANNELS), BF16)
    sources = (gate_query, gate_key, value_input, filter_taps, grad_output)
    blocks = pl.pallas_call(
        pack_kernel,
        out_shape=packed,
        in_specs=[far] * 5,
        out_specs=whole,
        scratch_shapes=[
            wide,
            wide,
            wide,
            pltpu.VMEM((GROUPS, ROWS), BF16),
            wide,
            turned,
            pltpu.SemaphoreType.DMA((5,)),
        ],
        compiler_params=small,
    )(*(pltpu.with_memory_space_constraint(source, pltpu.HBM) for source in sources))
    received = exchange(blocks)
    other = swap_cores(received)
    first, second, twist, last = (jnp.asarray(table) for table in tables())
    mixed = pl.pallas_call(
        own_kernel,
        out_shape=jax.ShapeDtypeStruct((2 * OUTER, SLOTS * ROWS), F32),
        in_specs=[scalar, whole, whole],
        out_specs=whole,
        compiler_params=pltpu.CompilerParams(vmem_limit_bytes=LARGE),
    )(core, received, first)
    results = pl.pallas_call(
        convolve_kernel,
        out_shape=packed,
        in_specs=[scalar] + [whole] * 6,
        out_specs=whole,
        compiler_params=pltpu.CompilerParams(vmem_limit_bytes=LARGE),
    )(core, other, mixed, first, second, twist, last)
    out = jax.ShapeDtypeStruct((ROWS, CHANNELS), BF16)
    return pl.pallas_call(
        finish_kernel,
        out_shape=(out, out, out, out, jax.ShapeDtypeStruct((GROUPS, ROWS), F32)),
        in_specs=[whole] * 5,
        out_specs=(whole,) * 5,
        scratch_shapes=[turned],
        compiler_params=small,
    )(exchange(results), gate_query, gate_key, value_input, grad_output)


def solution(mesh):
    rows = P(AXES, "chan")
    taps = P("chan", AXES)
    return jax.shard_map(
        per_device,
        mesh=mesh,
        in_specs=(rows, rows, rows, taps, rows),
        out_specs=(rows, rows, rows, rows, taps),
        check_vma=False,
    )
```

time: 65.5 us -> 56.9 us (0.87)
  the two profiles are of different devices: /device:TPU:1 before, /device:TPU:32 now
where the time goes in v2:
time: 56.9 us; the launch traced here: 56.7 us
  blocking collectives  50 us (88%)
  Pallas kernels  4.87 us (9%)
  local copies, waits for them, and re-layouts  1.09 us (2%)
  between operations  0.75 us (1%)
    all_to_all x2, blocking collectives, exchange(): lax.all_to_all(blocks.reshape(CHIPS * SLOTS, 1, ROWS), AXES, split_axis=0...  50 us
    pallas_call x1, Pallas kernels, per_device(): pl.pallas_call(convolve_kernel, out_shape=packed, in_specs=[scalar] + [wh...  2.25 us
    pallas_call x1, Pallas kernels, per_device(): pl.pallas_call(pack_kernel, out_shape=packed, in_specs=[far] * 5, out_spe...  1.25 us
  transfers between devices with their start and end apart: 1, of which 0 were waited for; matrix products, arithmetic and copies ran while one was open for 0% of the time, Pallas kernels for 1%

profile of v2, /device:TPU:32, one launch (start us, length us, event | category | flops | bytes accessed | tf_op | source)
XLA Modules:
  0.0 56.7 jit_solution(5163793908090168935)
XLA Ops:
  0.6 0.0 copy-start.1
  0.6 0.0 copy-start.2
  0.7 0.0 copy-start.3
  0.7 1.3 %shard_map.128 = f32[576,128]{1,0:T(8,128)S(1)} custom-call(bf16[128,256]{1,0:T(8,128)(2,1)} %query_ref.3, bf16[128,256]{1,0:T(8,128)(2,1)} %key_ref.3, bf16[128,256]{1,0:T(8,128)(2,1)} %value_ref.3, bf16[16,128]{1,0:T(8,128)(2,1)} %taps_ref.1, bf16[128,256]{1,0:T(8,128)(2,1)} %upstream_ref.3), custom_call_target="tpu_custom_call" | custom-call | tf_op jit(solution)/shard_map/pallas_call | solution.py:234
  1.9 29.3 %all_to_all.10 = f32[576,1,128]{2,1,0:T(1,128)S(1)} all-to-all(f32[576,1,128]{2,1,0:T(1,128)S(1)} %bitcast.11), channel_id=1, replica_groups={{0,4,8,12,16,20,24,28,32,36,40,44,48,52,56,60,64,68,72,76,80,84,88,92,9..., dimensions={0} | all-to-all | bytes 589824 | tf_op jit(solution)/shard_map/all_to_all | solution.py:214
  31.2 0.0 collective-permute-start
  31.2 0.0 copy-start
  31.2 1.0 %copy-done = bf16[2,512,192]{2,1,0:T(8,128)(2,1)S(1)} copy-done((bf16[2,512,192]{2,1,0:T(8,128)(2,1)S(1)}, bf16[2,512,192]{2,1,0:T(8,128)(2,1)}, u32[]{:S(2)}) %copy-start) | copy-done | bytes 393240
  32.3 0.5 shard_map.129.mixed_ref
  32.8 0.0 copy-start.4
  32.8 0.0 copy-start.5
  32.8 0.0 copy-start.6
  32.8 0.0 copy-start.7
  32.8 0.0 collective-permute-done.other_ref
  32.8 0.0 copy-done.1
  32.8 0.0 copy-done.2
  32.8 0.0 copy-done.3
  32.8 2.3 %shard_map.130 = f32[576,128]{1,0:T(8,128)S(1)} custom-call(s32[1]{0:T(128)} %bitcast.core_ref, f32[576,128]{1,0:T(8,128)S(1)} %collective-permute-done.other_ref, f32[512,1152]{1,0:T(8,128)S(1)} %shard_map.129.mixed_ref, bf16[2,512,192]{2,1,0:T(8,128)(2,1)S(1)} %copy-done, bf16[512,256]{1,0:T(8,128)(2,1)S(1)} %copy-done.3, f32[2,256,128]{2,1,0:T(8,128)S(1)} %copy-done.2, ...), custom_call_target="tpu_custom_call" | custom-call | tf_op jit(solution)/shard_map/pallas_call | solution.py:260
  35.1 20.7 %all_to_all.11 = f32[576,1,128]{2,1,0:T(1,128)S(1)} all-to-all(f32[576,1,128]{2,1,0:T(1,128)S(1)} %bitcast.9), channel_id=1, replica_groups={{0,4,8,12,16,20,24,28,32,36,40,44,48,52,56,60,64,68,72,76,80,84,88,92,9..., dimensions={0} | all-to-all | bytes 589824 | tf_op jit(solution)/shard_map/all_to_all | solution.py:214
  55.8 0.0 copy-done.4
  55.8 0.0 copy-done.5
  55.8 0.0 copy-done.6
  55.8 0.0 copy-done.7
  55.8 0.9 %shard_map.131 = (bf16[128,256]{1,0:T(8,128)(2,1)}, bf16[128,256]{1,0:T(8,128)(2,1)}, bf16[128,256]{1,0:T(8,128)(2,1)}, bf16[128,256]{1,0:T(8,128)(2,1)}, f32[16,128]{1,0:T(8,128)}) custom-call(f32[576,128]{1,0:T(8,128)S(1)} %bitcast.10, bf16[128,256]{1,0:T(8,128)(2,1)S(1)} %copy-done.4, bf16[128,256]{1,0:T(8,128)(2,1)S(1)} %copy-done.5, ...), custom_call_target="tpu_custom_call" | custom-call | tf_op jit(solution)/shard_map/pallas_call | solution.py:268
Async XLA Ops:
  0.6 32.2 %copy-start.1 = (bf16[2,128,512]{2,1,0:T(8,128)(2,1)S(1)}, bf16[2,128,512]{2,1,0:T(8,128)(2,1)}, u32[]{:S(2)}) copy-start(bf16[2,128,512]{2,1,0:T(8,128)(2,1)} %constant.30.clone.last_ref) | copy-start | bytes 786436
  0.6 32.2 %copy-start.2 = (f32[2,256,128]{2,1,0:T(8,128)S(1)}, f32[2,256,128]{2,1,0:T(8,128)}, u32[]{:S(2)}) copy-start(f32[2,256,128]{2,1,0:T(8,128)} %constant.29.clone.twist_ref) | copy-start | bytes 786436
  0.7 32.2 %copy-start.3 = (bf16[512,256]{1,0:T(8,128)(2,1)S(1)}, bf16[512,256]{1,0:T(8,128)(2,1)}, u32[]{:S(2)}) copy-start(bf16[512,256]{1,0:T(8,128)(2,1)} %constant.28.clone.second_ref) | copy-start | bytes 786436
  31.2 1.6 %collective-permute-start = (f32[576,128]{1,0:T(8,128)S(1)}, f32[576,128]{1,0:T(8,128)S(1)}, u32[]{:S(2)}, u32[]{:S(2)}) collective-permute-start(f32[576,128]{1,0:T(8,128)S(1)} %bitcast.12), channel_id=1, source_target_pairs={{0,2},{2,0},{4,6},{6,4},{8,10},{10,8},{12,14},{14,12},{1,3},{3,1},... | collective-permute-start | bytes 884744 | tf_op jit(solution)/shard_map/ppermute | solution.py:209
  31.2 1.0 %copy-start = (bf16[2,512,192]{2,1,0:T(8,128)(2,1)S(1)}, bf16[2,512,192]{2,1,0:T(8,128)(2,1)}, u32[]{:S(2)}) copy-start(bf16[2,512,192]{2,1,0:T(8,128)(2,1)} %constant.27.clone.first_ref) | copy-start | bytes 1179652
  32.8 23.1 %copy-start.4 = (bf16[128,256]{1,0:T(8,128)(2,1)S(1)}, bf16[128,256]{1,0:T(8,128)(2,1)}, u32[]{:S(2)}) copy-start(bf16[128,256]{1,0:T(8,128)(2,1)} %query_ref.3) | copy-start | bytes 196612
  32.8 23.0 %copy-start.5 = (bf16[128,256]{1,0:T(8,128)(2,1)S(1)}, bf16[128,256]{1,0:T(8,128)(2,1)}, u32[]{:S(2)}) copy-start(bf16[128,256]{1,0:T(8,128)(2,1)} %key_ref.3) | copy-start | bytes 196612
  32.8 23.0 %copy-start.6 = (bf16[128,256]{1,0:T(8,128)(2,1)S(1)}, bf16[128,256]{1,0:T(8,128)(2,1)}, u32[]{:S(2)}) copy-start(bf16[128,256]{1,0:T(8,128)(2,1)} %value_ref.3) | copy-start | bytes 196612
  32.8 23.0 %copy-start.7 = (bf16[128,256]{1,0:T(8,128)(2,1)S(1)}, bf16[128,256]{1,0:T(8,128)(2,1)}, u32[]{:S(2)}) copy-start(bf16[128,256]{1,0:T(8,128)(2,1)} %upstream_ref.3) | copy-start | bytes 196612

commit v3 on v2

v3 whole, which is shorter than its diff:
```python
import math

import jax
import jax.numpy as jnp
import numpy as np
from jax import lax
from jax.experimental import pallas as pl
from jax.experimental.pallas import tpu as pltpu
from jax.sharding import PartitionSpec as P

AXES = ("seq", "inner")
PIECES = 128
CHIPS = PIECES // 2
ROWS = 128
CHANNELS = 256
GROUPS = 16
SUBS = CHIPS // GROUPS
OWNED = 4
LENGTH = PIECES * ROWS
PADDED = 2 * LENGTH
OUTER = 2 * PIECES
GROUP_SLOT = 2 * OWNED
SCALE_SLOT = GROUP_SLOT + 1
SLOTS = SCALE_SLOT + 1
POWER = 48
RANGE = 125 / POWER
REACH = 2.0 ** (2 * RANGE) - 1.0
SMALL = 4 * 1024 * 1024
LARGE = 24 * 1024 * 1024
F32 = jnp.float32
BF16 = jnp.bfloat16


def split_table(table):
    high = table.astype(np.float32).astype(jnp.bfloat16)
    low = (table - high.astype(np.float64)).astype(jnp.bfloat16)
    return high, low


def tables():
    k1 = np.arange(OUTER)
    k1_half = np.arange(PIECES)
    t1 = np.stack((np.arange(0, PIECES, 2), np.arange(1, PIECES, 2)))
    t2 = np.arange(ROWS)
    outer = np.exp(-2j * np.pi * ((k1_half[None, :, None] * t1[:, None, :]) % OUTER) / OUTER)
    inner = np.exp(-2j * np.pi * ((t2[:, None] * t2[None, :]) % ROWS) / ROWS)
    twist = np.exp(-2j * np.pi * (k1[:, None] * t2[None, :]) / PADDED)
    first = np.concatenate((outer.real, outer.imag), axis=1)
    second = np.block([[inner.real, inner.imag], [-inner.imag, inner.real]])
    scale = 1.0 / (math.sqrt(LENGTH) * PADDED)
    last = np.swapaxes(np.concatenate((outer.real, outer.imag), axis=2), 1, 2) * scale
    first_high, first_low = split_table(first)
    second_high, second_low = split_table(second)
    last_high, last_low = split_table(last)
    return (
        np.concatenate((first_high, first_low, first_high), axis=2),
        np.concatenate((second_high, second_low), axis=0),
        np.stack((twist.real, twist.imag)).astype(np.float32),
        np.concatenate((last_high, last_low), axis=2),
    )


def split(values):
    high = values.astype(BF16)
    low = (values - high.astype(F32)).astype(BF16)
    return high, low


def dot(left, right):
    return jnp.dot(left, right, preferred_element_type=F32)


def scale_of(*arrays):
    peak = jnp.max(jnp.abs(arrays[0]), axis=(0, 1), keepdims=True)
    for array in arrays[1:]:
        peak = jnp.maximum(peak, jnp.max(jnp.abs(array), axis=(0, 1), keepdims=True))
    return (jnp.maximum(peak, 2.0**-118) * 1.0078125).astype(BF16).astype(F32)


def encode(values, scale):
    power = jnp.abs(values) * (REACH * 2.0**-RANGE / scale) + 2.0**-RANGE
    for _ in range(4):
        power = power * power
    power = power * (power * power)
    return jnp.where(values < 0, -power, power)


def decode(codes, scale):
    size = jnp.exp2(jnp.log2(jnp.abs(codes)) * (1.0 / POWER) + RANGE) - 1.0
    size = size * (scale * (1.0 / REACH))
    return jnp.where(codes < 0, -size, size)


def chip_rows(slot, first=0, count=CHIPS):
    return pl.ds(first * SLOTS + slot, count, stride=SLOTS)


def slot_of(array, owned):
    return 4 * (owned // 2) + 2 * array + owned % 2


def pack_kernel(
    query_ref, key_ref, value_ref, taps_ref, upstream_ref, out_ref, query, key, value, taps, upstream, turned, rows, sems
):
    moves = (
        (key_ref, key),
        (value_ref, value),
        (upstream_ref, upstream),
        (query_ref, query),
        (taps_ref, taps),
    )
    copies = [pltpu.make_async_copy(a, b, sems.at[i]) for i, (a, b) in enumerate(moves)]
    for copy in copies:
        copy.start()

    def place(array, left, right):
        product = left[...].astype(F32) * right[...].astype(F32)
        scale = scale_of(product)
        turned[array] = encode(jnp.transpose(product), scale)
        for owned in range(OWNED):
            for sub in range(SUBS):
                rows[chip_rows(slot_of(array, owned), GROUPS * sub, GROUPS), :] = turned[
                    array, pl.ds(SUBS * owned + sub, GROUPS, stride=GROUPS), :
                ]
        return scale

    copies[0].wait()
    copies[1].wait()
    value_scale = place(0, key, value)
    copies[2].wait()
    copies[3].wait()
    grad_scale = place(1, upstream, query)
    copies[4].wait()
    for sub in range(SUBS):
        rows[chip_rows(GROUP_SLOT, GROUPS * sub, GROUPS), :] = taps[...].astype(F32)
    lane = lax.broadcasted_iota(jnp.int32, (CHIPS, ROWS), 1)
    rows[chip_rows(SCALE_SLOT), :] = jnp.where(lane < ROWS // 2, value_scale, grad_scale)
    out_ref[...] = rows[...].astype(BF16)


def outer_forward(in_ref, rows, table):
    rows[...] = in_ref[...].astype(F32)
    scales = rows[chip_rows(SCALE_SLOT), :]
    value_scale, grad_scale = scales[:, :1], scales[:, ROWS // 2 : ROWS // 2 + 1]
    parts = [
        decode(rows[chip_rows(slot), :], grad_scale if slot % 4 > 1 else value_scale)
        for slot in range(GROUP_SLOT)
    ]
    high, low = split(jnp.concatenate(parts + [rows[chip_rows(GROUP_SLOT), :]], axis=1))
    mixed = dot(table, jnp.concatenate((high, high, low), axis=0))

    def part(half, slot):
        return mixed[half * PIECES : (half + 1) * PIECES, slot * ROWS : (slot + 1) * ROWS]

    results = [
        (part(0, slot) - part(1, slot + 1), part(1, slot) + part(0, slot + 1))
        for slot in range(0, 2 * OWNED, 2)
    ]
    return results + [(part(0, GROUP_SLOT), part(1, GROUP_SLOT))]


def own_kernel(core_ref, in_ref, first_ref, out_ref, rows):
    for index, (real, imag) in enumerate(outer_forward(in_ref, rows, first_ref[core_ref[0]])):
        out_ref[:, 2 * index * ROWS : (2 * index + 1) * ROWS] = real
        out_ref[:, (2 * index + 1) * ROWS : (2 * index + 2) * ROWS] = imag


def convolve_kernel(core_ref, other_ref, own_ref, first_ref, second_ref, twist_ref, last_ref, out_ref, rows):
    core = core_ref[0]
    sign = (1 - 2 * core).astype(F32)
    second = jnp.concatenate(
        (second_ref[: 2 * ROWS], second_ref[: 2 * ROWS], second_ref[2 * ROWS :]), axis=0
    )
    table = last_ref[core]
    last = jnp.concatenate((table[:, :PIECES], table[:, :PIECES], table[:, PIECES:]), axis=1)
    twist_real, twist_imag = twist_ref[0], twist_ref[1]

    def rotate(real, imag, sign):
        return (
            real * twist_real - sign * (imag * twist_imag),
            imag * twist_real + sign * (real * twist_imag),
        )

    def inner(real, imag):
        high, low = split(jnp.concatenate((real, imag), axis=1))
        result = dot(jnp.concatenate((high, low, high), axis=1), second)
        return result[:, :ROWS], result[:, ROWS:]

    def both(index, part, other):
        column = (2 * index + part) * ROWS
        own = own_ref[:, column : column + ROWS]
        return jnp.concatenate((own + other, sign * (own - other)), axis=0)

    def forward(index, real, imag):
        return inner(*rotate(both(index, 0, real), both(index, 1, imag), 1.0))

    def back(real, imag):
        turned_imag, turned_real = inner(imag, real)
        turned = jnp.concatenate(rotate(turned_real, turned_imag, -1.0), axis=1)
        return turned[:PIECES] + sign * turned[PIECES:]

    others = outer_forward(other_ref, rows, first_ref[1 - core])
    taps_real, taps_imag = forward(4, *others[4])
    spectra = []
    cross_real = cross_imag = None
    for pair in range(2):
        value_real, value_imag = forward(2 * pair, *others[2 * pair])
        spectra.append(
            back(
                value_real * taps_real - value_imag * taps_imag,
                value_real * taps_imag + value_imag * taps_real,
            )
        )
        grad_real, grad_imag = forward(2 * pair + 1, *others[2 * pair + 1])
        spectra.append(
            back(
                grad_real * taps_real + grad_imag * taps_imag,
                grad_imag * taps_real - grad_real * taps_imag,
            )
        )
        term_real = grad_real * value_real + grad_imag * value_imag
        term_imag = grad_imag * value_real - grad_real * value_imag
        cross_real = term_real if cross_real is None else cross_real + term_real
        cross_imag = term_imag if cross_imag is None else cross_imag + term_imag
    spectra.append(back(cross_real, cross_imag))
    high, low = split(jnp.concatenate(spectra, axis=1))
    final = dot(last, jnp.concatenate((high, low, high), axis=0))

    def block(half, index):
        return final[half * CHIPS : (half + 1) * CHIPS, index * ROWS : (index + 1) * ROWS]

    results = []
    for slot in range(0, GROUP_SLOT, 2):
        results.append(block(0, slot) + block(1, slot + 1))
        results.append(block(0, slot + 1) - block(1, slot))
    gfilter = block(0, GROUP_SLOT) + block(1, GROUP_SLOT + 1)
    causal_scale = scale_of(*(result for slot, result in enumerate(results) if slot % 4 < 2))
    back_scale = scale_of(*(result for slot, result in enumerate(results) if slot % 4 > 1))
    gfilter_scale = scale_of(gfilter)
    for slot, result in enumerate(results):
        rows[chip_rows(slot), :] = encode(result, back_scale if slot % 4 > 1 else causal_scale)
    rows[chip_rows(GROUP_SLOT), :] = encode(gfilter, gfilter_scale)
    lane = lax.broadcasted_iota(jnp.int32, (CHIPS, ROWS), 1)
    rows[chip_rows(SCALE_SLOT), :] = jnp.where(
        lane < ROWS // 4, causal_scale, jnp.where(lane < ROWS // 2, back_scale, gfilter_scale)
    )
    out_ref[...] = rows[...].astype(BF16)


def finish_kernel(
    in_ref,
    query_ref,
    key_ref,
    value_ref,
    upstream_ref,
    mixed_ref,
    gquery_ref,
    gkey_ref,
    gvalue_ref,
    gfilter_ref,
    mixed,
    gquery,
    gkey,
    gvalue,
    gfilter,
    turned,
    rows,
    sems,
):
    copies = []

    def send(source, target):
        copy = pltpu.make_async_copy(source, target, sems.at[len(copies)])
        copy.start()
        copies.append(copy)

    rows[...] = in_ref[...].astype(F32)
    scales = rows[chip_rows(SCALE_SLOT), :]

    def collect(array):
        scale = scales[:, array * ROWS // 4 : array * ROWS // 4 + 1]
        for owned in range(OWNED):
            values = decode(rows[chip_rows(slot_of(array, owned)), :], scale)
            for sub in range(SUBS):
                turned[array, pl.ds(SUBS * owned + sub, GROUPS, stride=GROUPS), :] = values[
                    GROUPS * sub : GROUPS * (sub + 1)
                ]
        return jnp.transpose(turned[array])

    causal = collect(0)
    mixed[...] = (query_ref[...].astype(F32) * causal).astype(BF16)
    send(mixed, mixed_ref)
    gquery[...] = (upstream_ref[...].astype(F32) * causal).astype(BF16)
    send(gquery, gquery_ref)
    back_conv = collect(1)
    gkey[...] = (back_conv * value_ref[...].astype(F32)).astype(BF16)
    send(gkey, gkey_ref)
    gvalue[...] = (back_conv * key_ref[...].astype(F32)).astype(BF16)
    send(gvalue, gvalue_ref)
    shares = decode(rows[chip_rows(GROUP_SLOT), :], scales[:, ROWS // 2 : ROWS // 2 + 1])
    parts = [shares[GROUPS * sub : GROUPS * (sub + 1)] for sub in range(SUBS)]
    gfilter[...] = (parts[0] + parts[1]) + (parts[2] + parts[3])
    send(gfilter, gfilter_ref)
    for copy in copies:
        copy.wait()


def swap_cores(values):
    count = lax.axis_size("inner")
    return lax.ppermute(values, "inner", [(i, i ^ 1) for i in range(count)])


def exchange(blocks):
    groups = [list(range(core, PIECES, 2)) for core in range(2)]
    return lax.all_to_all(
        blocks.reshape(CHIPS * SLOTS // 2, 2, ROWS),
        AXES,
        split_axis=0,
        concat_axis=0,
        tiled=True,
        axis_index_groups=groups,
    ).reshape(CHIPS * SLOTS, ROWS)


def per_device(gate_query, gate_key, value_input, filter_taps, grad_output):
    core = (lax.axis_index("inner") % 2).astype(jnp.int32).reshape(1)
    scalar = pl.BlockSpec(memory_space=pltpu.SMEM)
    whole = pl.BlockSpec(memory_space=pltpu.VMEM)
    small = pltpu.CompilerParams(vmem_limit_bytes=SMALL)
    packed = jax.ShapeDtypeStruct((CHIPS * SLOTS, ROWS), BF16)
    rows = pltpu.VMEM((CHIPS * SLOTS, ROWS), F32)
    turned = pltpu.VMEM((2, CHANNELS, ROWS), F32)
    far = pl.BlockSpec(memory_space=pltpu.HBM)
    wide = pltpu.VMEM((ROWS, CHANNELS), BF16)
    sources = (gate_query, gate_key, value_input, filter_taps, grad_output)
    blocks = pl.pallas_call(
        pack_kernel,
        out_shape=packed,
        in_specs=[far] * 5,
        out_specs=whole,
        scratch_shapes=[
            wide,
            wide,
            wide,
            pltpu.VMEM((GROUPS, ROWS), BF16),
            wide,
            turned,
            rows,
            pltpu.SemaphoreType.DMA((5,)),
        ],
        compiler_params=small,
    )(*(pltpu.with_memory_space_constraint(source, pltpu.HBM) for source in sources))
    received = exchange(blocks)
    other = swap_cores(received)
    first, second, twist, last = (jnp.asarray(table) for table in tables())
    own = pl.pallas_call(
        own_kernel,
        out_shape=jax.ShapeDtypeStruct((PIECES, SLOTS * ROWS), F32),
        in_specs=[scalar, whole, whole],
        out_specs=whole,
        scratch_shapes=[rows],
        compiler_params=pltpu.CompilerParams(vmem_limit_bytes=LARGE),
    )(core, received, first)
    results = pl.pallas_call(
        convolve_kernel,
        out_shape=packed,
        in_specs=[scalar] + [whole] * 6,
        out_specs=whole,
        scratch_shapes=[rows],
        compiler_params=pltpu.CompilerParams(vmem_limit_bytes=LARGE),
    )(core, other, own, first, second, twist, last)
    out = jax.ShapeDtypeStruct((ROWS, CHANNELS), BF16)
    return pl.pallas_call(
        finish_kernel,
        out_shape=(out, out, out, out, jax.ShapeDtypeStruct((GROUPS, ROWS), F32)),
        in_specs=[whole] * 5,
        out_specs=(far,) * 5,
        scratch_shapes=[
            wide,
            wide,
            wide,
            wide,
            pltpu.VMEM((GROUPS, ROWS), F32),
            turned,
            rows,
            pltpu.SemaphoreType.DMA((5,)),
        ],
        compiler_params=small,
    )(exchange(results), gate_query, gate_key, value_input, grad_output)


def solution(mesh):
    rows = P(AXES, "chan")
    taps = P("chan", AXES)
    return jax.shard_map(
        per_device,
        mesh=mesh,
        in_specs=(rows, rows, rows, taps, rows),
        out_specs=(rows, rows, rows, rows, taps),
        check_vma=False,
    )
```

time: 56.9 us -> 51.7 us (0.909)
  the two profiles are of different devices: /device:TPU:32 before, /device:TPU:1 now
where the time goes in v3:
time: 51.7 us; the launch traced here: 51.3 us
  blocking collectives  42.4 us (82%)
  Pallas kernels  5.2 us (10%)
  starting transfers between devices  2.41 us (5%)
  between operations  0.71 us (1%)
  waiting for transfers between devices  0.58 us (1%)
    all_to_all x2, blocking collectives, exchange(): lax.all_to_all(blocks.reshape(CHIPS * SLOTS // 2, 2, ROWS), AXES, split_a...  42.4 us
    ppermute x1, starting transfers between devices, swap_cores(): return lax.ppermute(values, 'inner', [(i, i ^ 1) for i in range(count)])  2.41 us
    pallas_call x1, Pallas kernels, per_device(): pl.pallas_call(convolve_kernel, out_shape=packed, in_specs=[scalar] + [wh...  2.34 us
    pallas_call x1, Pallas kernels, per_device(): pl.pallas_call(pack_kernel, out_shape=packed, in_specs=[far] * 5, out_spe...  1.41 us
  transfers between devices with their start and end apart: 1, of which 1 were waited for; matrix products, arithmetic and copies ran while one was open for 0% of the time, Pallas kernels for 1%

profile of v3, /device:TPU:1, one launch (start us, length us, event | category | flops | bytes accessed | tf_op | source)
XLA Modules:
  0.0 51.3 jit_solution(146798968876878277)
XLA Ops:
  0.6 1.4 %shard_map.128 = bf16[640,128]{1,0:T(8,128)(2,1)S(1)} custom-call(bf16[128,256]{1,0:T(8,128)(2,1)} %query_ref.3, bf16[128,256]{1,0:T(8,128)(2,1)} %key_ref.3, bf16[128,256]{1,0:T(8,128)(2,1)} %value_ref.3, bf16[16,128]{1,0:T(8,128)(2,1)} %taps_ref.1, bf16[128,256]{1,0:T(8,128)(2,1)} %upstream_ref.3), custom_call_target="tpu_custom_call" | custom-call | tf_op jit(solution)/shard_map/pallas_call | solution.py:336
  2.0 0.0 copy-start
  2.1 26.7 %all_to_all.10 = bf16[320,2,128]{2,1,0:T(2,128)(2,1)S(1)} all-to-all(bf16[320,2,128]{2,1,0:T(2,128)(2,1)S(1)} %bitcast.6), channel_id=1, replica_groups={{0,4,8,12,16,20,24,28,32,36,40,44,48,52,56,60,64,68,72,76,80,84,88,92,9..., dimensions={0} | all-to-all | bytes 327680 | tf_op jit(solution)/shard_map/all_to_all | solution.py:315
  28.8 2.4 %collective-permute-start = (bf16[640,128]{1,0:T(8,128)(2,1)S(1)}, bf16[640,128]{1,0:T(8,128)(2,1)S(1)}, u32[]{:S(2)}, u32[]{:S(2)}) collective-permute-start(bf16[640,128]{1,0:T(8,128)(2,1)S(1)} %bitcast.7), channel_id=1, source_target_pairs={{0,2},{2,0},{4,6},{6,4},{8,10},{10,8},{12,14},{14,12},{1,3},{3,1},... | collective-permute-start | bytes 491528 | tf_op jit(solution)/shard_map/ppermute | solution.py:310
  31.2 0.0 copy-done
  31.2 0.0 copy-start.1
  31.2 0.0 copy-start.2
  31.2 0.0 copy-start.7
  31.2 0.4 shard_map.129.own_ref
  31.6 0.6 %collective-permute-done.other_ref = bf16[640,128]{1,0:T(8,128)(2,1)S(1)} collective-permute-done((bf16[640,128]{1,0:T(8,128)(2,1)S(1)}, bf16[640,128]{1,0:T(8,128)(2,1)S(1)}, u32[]{:S(2)}, u32[]{:S(2)}) %collective-permute-start) | collective-permute-done | bytes 163872 | tf_op jit(solution)/shard_map/ppermute | solution.py:310
  32.2 0.0 copy-done.1
  32.2 0.0 copy-done.2
  32.2 0.0 copy-done.7
  32.2 2.3 %shard_map.130 = bf16[640,128]{1,0:T(8,128)(2,1)S(1)} custom-call(s32[1]{0:T(128)} %bitcast.core_ref, bf16[640,128]{1,0:T(8,128)(2,1)S(1)} %collective-permute-done.other_ref, f32[128,1280]{1,0:T(8,128)S(1)} %shard_map.129.own_ref, bf16[2,256,192]{2,1,0:T(8,128)(2,1)S(1)} %copy-done, bf16[512,256]{1,0:T(8,128)(2,1)S(1)} %copy-done.2, ...), custom_call_target="tpu_custom_call" | custom-call | tf_op jit(solution)/shard_map/pallas_call | solution.py:364
  34.6 0.0 copy-start.3
  34.6 0.0 copy-start.4
  34.6 0.0 copy-start.5
  34.6 0.0 copy-start.6
  34.6 15.7 %all_to_all.11 = bf16[320,2,128]{2,1,0:T(2,128)(2,1)S(1)} all-to-all(bf16[320,2,128]{2,1,0:T(2,128)(2,1)S(1)} %bitcast.9), channel_id=1, replica_groups={{0,4,8,12,16,20,24,28,32,36,40,44,48,52,56,60,64,68,72,76,80,84,88,92,9..., dimensions={0} | all-to-all | bytes 327680 | tf_op jit(solution)/shard_map/all_to_all | solution.py:315
  50.3 0.0 copy-done.3
  50.3 0.0 copy-done.4
  50.3 0.0 copy-done.5
  50.3 0.0 copy-done.6
  50.3 1.0 %shard_map.131 = (bf16[128,256]{1,0:T(8,128)(2,1)}, bf16[128,256]{1,0:T(8,128)(2,1)}, bf16[128,256]{1,0:T(8,128)(2,1)}, bf16[128,256]{1,0:T(8,128)(2,1)}, f32[16,128]{1,0:T(8,128)}) custom-call(bf16[640,128]{1,0:T(8,128)(2,1)S(1)} %bitcast.5, bf16[128,256]{1,0:T(8,128)(2,1)S(1)} %copy-done.3, bf16[128,256]{1,0:T(8,128)(2,1)S(1)} %copy-done.4, ...), custom_call_target="tpu_custom_call" | custom-call | tf_op jit(solution)/shard_map/pallas_call | solution.py:373
Async XLA Ops:
  2.0 29.1 %copy-start = (bf16[2,256,192]{2,1,0:T(8,128)(2,1)S(1)}, bf16[2,256,192]{2,1,0:T(8,128)(2,1)}, u32[]{:S(2)}) copy-start(bf16[2,256,192]{2,1,0:T(8,128)(2,1)} %constant.27.clone.first_ref) | copy-start | bytes 589828
  28.8 3.4 %collective-permute-start = (bf16[640,128]{1,0:T(8,128)(2,1)S(1)}, bf16[640,128]{1,0:T(8,128)(2,1)S(1)}, u32[]{:S(2)}, u32[]{:S(2)}) collective-permute-start(bf16[640,128]{1,0:T(8,128)(2,1)S(1)} %bitcast.7), channel_id=1, source_target_pairs={{0,2},{2,0},{4,6},{6,4},{8,10},{10,8},{12,14},{14,12},{1,3},{3,1},... | collective-permute-start | bytes 491528 | tf_op jit(solution)/shard_map/ppermute | solution.py:310
  31.2 1.0 %copy-start.1 = (f32[2,256,128]{2,1,0:T(8,128)S(1)}, f32[2,256,128]{2,1,0:T(8,128)}, u32[]{:S(2)}) copy-start(f32[2,256,128]{2,1,0:T(8,128)} %constant.29.clone.twist_ref) | copy-start | bytes 786436
  31.2 1.0 %copy-start.2 = (bf16[512,256]{1,0:T(8,128)(2,1)S(1)}, bf16[512,256]{1,0:T(8,128)(2,1)}, u32[]{:S(2)}) copy-start(bf16[512,256]{1,0:T(8,128)(2,1)} %constant.28.clone.second_ref) | copy-start | bytes 786436
  31.2 1.1 %copy-start.7 = (bf16[2,128,256]{2,1,0:T(8,128)(2,1)S(1)}, bf16[2,128,256]{2,1,0:T(8,128)(2,1)}, u32[]{:S(2)}) copy-start(bf16[2,128,256]{2,1,0:T(8,128)(2,1)} %constant.30.clone.last_ref) | copy-start | bytes 393220
  34.6 15.7 %copy-start.3 = (bf16[128,256]{1,0:T(8,128)(2,1)S(1)}, bf16[128,256]{1,0:T(8,128)(2,1)}, u32[]{:S(2)}) copy-start(bf16[128,256]{1,0:T(8,128)(2,1)} %query_ref.3) | copy-start | bytes 196612
  34.6 15.7 %copy-start.4 = (bf16[128,256]{1,0:T(8,128)(2,1)S(1)}, bf16[128,256]{1,0:T(8,128)(2,1)}, u32[]{:S(2)}) copy-start(bf16[128,256]{1,0:T(8,128)(2,1)} %key_ref.3) | copy-start | bytes 196612
  34.6 15.7 %copy-start.5 = (bf16[128,256]{1,0:T(8,128)(2,1)S(1)}, bf16[128,256]{1,0:T(8,128)(2,1)}, u32[]{:S(2)}) copy-start(bf16[128,256]{1,0:T(8,128)(2,1)} %value_ref.3) | copy-start | bytes 196612
  34.6 15.7 %copy-start.6 = (bf16[128,256]{1,0:T(8,128)(2,1)S(1)}, bf16[128,256]{1,0:T(8,128)(2,1)}, u32[]{:S(2)}) copy-start(bf16[128,256]{1,0:T(8,128)(2,1)} %upstream_ref.3) | copy-start | bytes 196612

commit v4 on v3

--- a/solution.py
+++ b/solution.py
@@ -22,9 +22,10 @@
 GROUP_SLOT = 2 * OWNED
 SCALE_SLOT = GROUP_SLOT + 1
 SLOTS = SCALE_SLOT + 1
-POWER = 48
+POWER = 64
 RANGE = 125 / POWER
 REACH = 2.0 ** (2 * RANGE) - 1.0
+SHARE = 8
 SMALL = 4 * 1024 * 1024
 LARGE = 24 * 1024 * 1024
 F32 = jnp.float32
@@ -70,19 +71,28 @@
     return jnp.dot(left, right, preferred_element_type=F32)
 
 
-def scale_of(*arrays):
-    peak = jnp.max(jnp.abs(arrays[0]), axis=(0, 1), keepdims=True)
-    for array in arrays[1:]:
-        peak = jnp.maximum(peak, jnp.max(jnp.abs(array), axis=(0, 1), keepdims=True))
+def scale_of(values):
+    peak = jnp.max(jnp.abs(values), axis=1, keepdims=True)
     return (jnp.maximum(peak, 2.0**-118) * 1.0078125).astype(BF16).astype(F32)
 
 
 def encode(values, scale):
     power = jnp.abs(values) * (REACH * 2.0**-RANGE / scale) + 2.0**-RANGE
-    for _ in range(4):
+    for _ in range(6):
         power = power * power
-    power = power * (power * power)
     return jnp.where(values < 0, -power, power)
+
+
+def scale_at(scales, slot):
+    return scales[:, SHARE * slot : SHARE * slot + 1]
+
+
+def join_scales(scales):
+    lane = lax.broadcasted_iota(jnp.int32, (scales[0].shape[0], ROWS), 1)
+    joined = scales[0]
+    for slot, scale in enumerate(scales[1:], 1):
+        joined = jnp.where(lane < SHARE * slot, joined, scale)
+    return joined
 
 
 def decode(codes, scale):
@@ -100,7 +110,7 @@
 
 
 def pack_kernel(
-    query_ref, key_ref, value_ref, taps_ref, upstream_ref, out_ref, query, key, value, taps, upstream, turned, rows, sems
+    query_ref, key_ref, value_ref, taps_ref, upstream_ref, out_ref, query, key, value, taps, upstream, turned, scaled, rows, sems
 ):
     moves = (
         (key_ref, key),
@@ -115,36 +125,40 @@
 
     def place(array, left, right):
         product = left[...].astype(F32) * right[...].astype(F32)
-        scale = scale_of(product)
-        turned[array] = encode(jnp.transpose(product), scale)
+        values = jnp.transpose(product)
+        scale = scale_of(values)
+        turned[array] = encode(values, scale)
+        scaled[array] = jnp.broadcast_to(scale, (CHANNELS, ROWS))
         for owned in range(OWNED):
             for sub in range(SUBS):
                 rows[chip_rows(slot_of(array, owned), GROUPS * sub, GROUPS), :] = turned[
                     array, pl.ds(SUBS * owned + sub, GROUPS, stride=GROUPS), :
                 ]
-        return scale
 
     copies[0].wait()
     copies[1].wait()
-    value_scale = place(0, key, value)
+    place(0, key, value)
     copies[2].wait()
     copies[3].wait()
-    grad_scale = place(1, upstream, query)
+    place(1, upstream, query)
     copies[4].wait()
     for sub in range(SUBS):
         rows[chip_rows(GROUP_SLOT, GROUPS * sub, GROUPS), :] = taps[...].astype(F32)
-    lane = lax.broadcasted_iota(jnp.int32, (CHIPS, ROWS), 1)
-    rows[chip_rows(SCALE_SLOT), :] = jnp.where(lane < ROWS // 2, value_scale, grad_scale)
+        scales = [None] * GROUP_SLOT
+        for array in range(2):
+            for owned in range(OWNED):
+                scales[slot_of(array, owned)] = scaled[
+                    array, pl.ds(SUBS * owned + sub, GROUPS, stride=GROUPS), :
+                ]
+        rows[chip_rows(SCALE_SLOT, GROUPS * sub, GROUPS), :] = join_scales(scales)
     out_ref[...] = rows[...].astype(BF16)
 
 
 def outer_forward(in_ref, rows, table):
     rows[...] = in_ref[...].astype(F32)
     scales = rows[chip_rows(SCALE_SLOT), :]
-    value_scale, grad_scale = scales[:, :1], scales[:, ROWS // 2 : ROWS // 2 + 1]
     parts = [
-        decode(rows[chip_rows(slot), :], grad_scale if slot % 4 > 1 else value_scale)
-        for slot in range(GROUP_SLOT)
+        decode(rows[chip_rows(slot), :], scale_at(scales, slot)) for slot in range(GROUP_SLOT)
     ]
     high, low = split(jnp.concatenate(parts + [rows[chip_rows(GROUP_SLOT), :]], axis=1))
     mixed = dot(table, jnp.concatenate((high, high, low), axis=0))
@@ -233,16 +247,12 @@
     for slot in range(0, GROUP_SLOT, 2):
         results.append(block(0, slot) + block(1, slot + 1))
         results.append(block(0, slot + 1) - block(1, slot))
-    gfilter = block(0, GROUP_SLOT) + block(1, GROUP_SLOT + 1)
-    causal_scale = scale_of(*(result for slot, result in enumerate(results) if slot % 4 < 2))
-    back_scale = scale_of(*(result for slot, result in enumerate(results) if slot % 4 > 1))
-    gfilter_scale = scale_of(gfilter)
+    results.append(block(0, GROUP_SLOT) + block(1, GROUP_SLOT + 1))
+    scales = [scale_of(result) for result in results]
     for slot, result in enumerate(results):
-        rows[chip_rows(slot), :] = encode(result, back_scale if slot % 4 > 1 else causal_scale)
-    rows[chip_rows(GROUP_SLOT), :] = encode(gfilter, gfilter_scale)
-    lane = lax.broadcasted_iota(jnp.int32, (CHIPS, ROWS), 1)
-    rows[chip_rows(SCALE_SLOT), :] = jnp.where(
-        lane < ROWS // 4, causal_scale, jnp.where(lane < ROWS // 2, back_scale, gfilter_scale)
+        rows[chip_rows(slot), :] = encode(result, scales[slot])
+    rows[chip_rows(SCALE_SLOT), :] = join_scales(
+        [jnp.broadcast_to(scale, (CHIPS, ROWS)) for scale in scales]
     )
     out_ref[...] = rows[...].astype(BF16)
 
@@ -278,9 +288,9 @@
     scales = rows[chip_rows(SCALE_SLOT), :]
 
     def collect(array):
-        scale = scales[:, array * ROWS // 4 : array * ROWS // 4 + 1]
         for owned in range(OWNED):
-            values = decode(rows[chip_rows(slot_of(array, owned)), :], scale)
+            slot = slot_of(array, owned)
+            values = decode(rows[chip_rows(slot), :], scale_at(scales, slot))
             for sub in range(SUBS):
                 turned[array, pl.ds(SUBS * owned + sub, GROUPS, stride=GROUPS), :] = values[
                     GROUPS * sub : GROUPS * (sub + 1)
@@ -297,7 +307,7 @@
     send(gkey, gkey_ref)
     gvalue[...] = (back_conv * key_ref[...].astype(F32)).astype(BF16)
     send(gvalue, gvalue_ref)
-    shares = decode(rows[chip_rows(GROUP_SLOT), :], scales[:, ROWS // 2 : ROWS // 2 + 1])
+    shares = decode(rows[chip_rows(GROUP_SLOT), :], scale_at(scales, GROUP_SLOT))
     parts = [shares[GROUPS * sub : GROUPS * (sub + 1)] for sub in range(SUBS)]
     gfilter[...] = (parts[0] + parts[1]) + (parts[2] + parts[3])
     send(gfilter, gfilter_ref)
@@ -344,6 +354,7 @@
             wide,
             pltpu.VMEM((GROUPS, ROWS), BF16),
             wide,
+            turned,
             turned,
             rows,
             pltpu.SemaphoreType.DMA((5,)),

time: 51.7 us -> 51.7 us (level)
  no operation moved by 1% of the time
where the time goes in v4:
time: 51.7 us; the launch traced here: 51.3 us
  blocking collectives  42.4 us (82%)
  Pallas kernels  5.26 us (10%)
  starting transfers between devices  2.41 us (5%)
  between operations  0.71 us (1%)
  waiting for transfers between devices  0.55 us (1%)
    all_to_all x2, blocking collectives, exchange(): lax.all_to_all(blocks.reshape(CHIPS * SLOTS // 2, 2, ROWS), AXES, split_a...  42.4 us
    ppermute x1, starting transfers between devices, swap_cores(): return lax.ppermute(values, 'inner', [(i, i ^ 1) for i in range(count)])  2.41 us
    pallas_call x1, Pallas kernels, per_device(): pl.pallas_call(convolve_kernel, out_shape=packed, in_specs=[scalar] + [wh...  2.26 us
    pallas_call x1, Pallas kernels, per_device(): pl.pallas_call(pack_kernel, out_shape=packed, in_specs=[far] * 5, out_spe...  1.54 us
  transfers between devices with their start and end apart: 1, of which 1 were waited for; matrix products, arithmetic and copies ran while one was open for 0% of the time, Pallas kernels for 1%

profile of v4, /device:TPU:1, one launch (start us, length us, event | category | flops | bytes accessed | tf_op | source)
XLA Modules:
  0.0 51.3 jit_solution(10548258132239618170)
XLA Ops:
  0.6 1.5 %shard_map.128 = bf16[640,128]{1,0:T(8,128)(2,1)S(1)} custom-call(bf16[128,256]{1,0:T(8,128)(2,1)} %query_ref.3, bf16[128,256]{1,0:T(8,128)(2,1)} %key_ref.3, bf16[128,256]{1,0:T(8,128)(2,1)} %value_ref.3, bf16[16,128]{1,0:T(8,128)(2,1)} %taps_ref.1, bf16[128,256]{1,0:T(8,128)(2,1)} %upstream_ref.3), custom_call_target="tpu_custom_call" | custom-call | tf_op jit(solution)/shard_map/pallas_call | solution.py:346
  2.2 0.0 copy-start
  2.2 26.7 %all_to_all.10 = bf16[320,2,128]{2,1,0:T(2,128)(2,1)S(1)} all-to-all(bf16[320,2,128]{2,1,0:T(2,128)(2,1)S(1)} %bitcast.6), channel_id=1, replica_groups={{0,4,8,12,16,20,24,28,32,36,40,44,48,52,56,60,64,68,72,76,80,84,88,92,9..., dimensions={0} | all-to-all | bytes 327680 | tf_op jit(solution)/shard_map/all_to_all | solution.py:325
  28.9 2.4 %collective-permute-start = (bf16[640,128]{1,0:T(8,128)(2,1)S(1)}, bf16[640,128]{1,0:T(8,128)(2,1)S(1)}, u32[]{:S(2)}, u32[]{:S(2)}) collective-permute-start(bf16[640,128]{1,0:T(8,128)(2,1)S(1)} %bitcast.7), channel_id=1, source_target_pairs={{0,2},{2,0},{4,6},{6,4},{8,10},{10,8},{12,14},{14,12},{1,3},{3,1},... | collective-permute-start | bytes 491528 | tf_op jit(solution)/shard_map/ppermute | solution.py:320
  31.3 0.0 copy-done
  31.3 0.0 copy-start.1
  31.3 0.0 copy-start.2
  31.3 0.0 copy-start.7
  31.3 0.5 shard_map.129.own_ref
  31.8 0.5 %collective-permute-done.other_ref = bf16[640,128]{1,0:T(8,128)(2,1)S(1)} collective-permute-done((bf16[640,128]{1,0:T(8,128)(2,1)S(1)}, bf16[640,128]{1,0:T(8,128)(2,1)S(1)}, u32[]{:S(2)}, u32[]{:S(2)}) %collective-permute-start) | collective-permute-done | bytes 163872 | tf_op jit(solution)/shard_map/ppermute | solution.py:320
  32.3 0.0 copy-done.1
  32.3 0.0 copy-done.2
  32.3 0.0 copy-done.7
  32.4 2.3 %shard_map.130 = bf16[640,128]{1,0:T(8,128)(2,1)S(1)} custom-call(s32[1]{0:T(128)} %bitcast.core_ref, bf16[640,128]{1,0:T(8,128)(2,1)S(1)} %collective-permute-done.other_ref, f32[128,1280]{1,0:T(8,128)S(1)} %shard_map.129.own_ref, bf16[2,256,192]{2,1,0:T(8,128)(2,1)S(1)} %copy-done, bf16[512,256]{1,0:T(8,128)(2,1)S(1)} %copy-done.2, ...), custom_call_target="tpu_custom_call" | custom-call | tf_op jit(solution)/shard_map/pallas_call | solution.py:375
  34.6 0.0 copy-start.3
  34.6 0.0 copy-start.4
  34.6 0.0 copy-start.5
  34.6 0.0 copy-start.6
  34.7 15.7 %all_to_all.11 = bf16[320,2,128]{2,1,0:T(2,128)(2,1)S(1)} all-to-all(bf16[320,2,128]{2,1,0:T(2,128)(2,1)S(1)} %bitcast.9), channel_id=1, replica_groups={{0,4,8,12,16,20,24,28,32,36,40,44,48,52,56,60,64,68,72,76,80,84,88,92,9..., dimensions={0} | all-to-all | bytes 327680 | tf_op jit(solution)/shard_map/all_to_all | solution.py:325
  50.3 0.0 copy-done.3
  50.3 0.0 copy-done.4
  50.3 0.0 copy-done.5
  50.3 0.0 copy-done.6
  50.3 1.0 %shard_map.131 = (bf16[128,256]{1,0:T(8,128)(2,1)}, bf16[128,256]{1,0:T(8,128)(2,1)}, bf16[128,256]{1,0:T(8,128)(2,1)}, bf16[128,256]{1,0:T(8,128)(2,1)}, f32[16,128]{1,0:T(8,128)}) custom-call(bf16[640,128]{1,0:T(8,128)(2,1)S(1)} %bitcast.5, bf16[128,256]{1,0:T(8,128)(2,1)S(1)} %copy-done.3, bf16[128,256]{1,0:T(8,128)(2,1)S(1)} %copy-done.4, ...), custom_call_target="tpu_custom_call" | custom-call | tf_op jit(solution)/shard_map/pallas_call | solution.py:384
Async XLA Ops:
  2.2 29.1 %copy-start = (bf16[2,256,192]{2,1,0:T(8,128)(2,1)S(1)}, bf16[2,256,192]{2,1,0:T(8,128)(2,1)}, u32[]{:S(2)}) copy-start(bf16[2,256,192]{2,1,0:T(8,128)(2,1)} %constant.27.clone.first_ref) | copy-start | bytes 589828
  28.9 3.4 %collective-permute-start = (bf16[640,128]{1,0:T(8,128)(2,1)S(1)}, bf16[640,128]{1,0:T(8,128)(2,1)S(1)}, u32[]{:S(2)}, u32[]{:S(2)}) collective-permute-start(bf16[640,128]{1,0:T(8,128)(2,1)S(1)} %bitcast.7), channel_id=1, source_target_pairs={{0,2},{2,0},{4,6},{6,4},{8,10},{10,8},{12,14},{14,12},{1,3},{3,1},... | collective-permute-start | bytes 491528 | tf_op jit(solution)/shard_map/ppermute | solution.py:320
  31.3 1.0 %copy-start.1 = (f32[2,256,128]{2,1,0:T(8,128)S(1)}, f32[2,256,128]{2,1,0:T(8,128)}, u32[]{:S(2)}) copy-start(f32[2,256,128]{2,1,0:T(8,128)} %constant.29.clone.twist_ref) | copy-start | bytes 786436
  31.3 1.0 %copy-start.2 = (bf16[512,256]{1,0:T(8,128)(2,1)S(1)}, bf16[512,256]{1,0:T(8,128)(2,1)}, u32[]{:S(2)}) copy-start(bf16[512,256]{1,0:T(8,128)(2,1)} %constant.28.clone.second_ref) | copy-start | bytes 786436
  31.3 1.1 %copy-start.7 = (bf16[2,128,256]{2,1,0:T(8,128)(2,1)S(1)}, bf16[2,128,256]{2,1,0:T(8,128)(2,1)}, u32[]{:S(2)}) copy-start(bf16[2,128,256]{2,1,0:T(8,128)(2,1)} %constant.30.clone.last_ref) | copy-start | bytes 393220
  34.6 15.7 %copy-start.3 = (bf16[128,256]{1,0:T(8,128)(2,1)S(1)}, bf16[128,256]{1,0:T(8,128)(2,1)}, u32[]{:S(2)}) copy-start(bf16[128,256]{1,0:T(8,128)(2,1)} %query_ref.3) | copy-start | bytes 196612
  34.6 15.7 %copy-start.4 = (bf16[128,256]{1,0:T(8,128)(2,1)S(1)}, bf16[128,256]{1,0:T(8,128)(2,1)}, u32[]{:S(2)}) copy-start(bf16[128,256]{1,0:T(8,128)(2,1)} %key_ref.3) | copy-start | bytes 196612
  34.6 15.7 %copy-start.5 = (bf16[128,256]{1,0:T(8,128)(2,1)S(1)}, bf16[128,256]{1,0:T(8,128)(2,1)}, u32[]{:S(2)}) copy-start(bf16[128,256]{1,0:T(8,128)(2,1)} %value_ref.3) | copy-start | bytes 196612
  34.6 15.7 %copy-start.6 = (bf16[128,256]{1,0:T(8,128)(2,1)S(1)}, bf16[128,256]{1,0:T(8,128)(2,1)}, u32[]{:S(2)}) copy-start(bf16[128,256]{1,0:T(8,128)(2,1)} %upstream_ref.3) | copy-start | bytes 196612

commit v5 on v4

--- a/solution.py
+++ b/solution.py
@@ -71,8 +71,8 @@
     return jnp.dot(left, right, preferred_element_type=F32)
 
 
-def scale_of(values):
-    peak = jnp.max(jnp.abs(values), axis=1, keepdims=True)
+def scale_of(values, axis):
+    peak = jnp.max(jnp.abs(values), axis=axis, keepdims=True)
     return (jnp.maximum(peak, 2.0**-118) * 1.0078125).astype(BF16).astype(F32)
 
 
@@ -125,10 +125,11 @@
 
     def place(array, left, right):
         product = left[...].astype(F32) * right[...].astype(F32)
-        values = jnp.transpose(product)
-        scale = scale_of(values)
-        turned[array] = encode(values, scale)
-        scaled[array] = jnp.broadcast_to(scale, (CHANNELS, ROWS))
+        scale = scale_of(product, axis=0)
+        codes = encode(product, scale).astype(BF16)
+        turned[array] = jnp.transpose(codes).astype(F32)
+        wide_scale = jnp.broadcast_to(scale.astype(BF16), (ROWS, CHANNELS))
+        scaled[array] = jnp.transpose(wide_scale).astype(F32)
         for owned in range(OWNED):
             for sub in range(SUBS):
                 rows[chip_rows(slot_of(array, owned), GROUPS * sub, GROUPS), :] = turned[
@@ -157,20 +158,21 @@
 def outer_forward(in_ref, rows, table):
     rows[...] = in_ref[...].astype(F32)
     scales = rows[chip_rows(SCALE_SLOT), :]
-    parts = [
-        decode(rows[chip_rows(slot), :], scale_at(scales, slot)) for slot in range(GROUP_SLOT)
-    ]
-    high, low = split(jnp.concatenate(parts + [rows[chip_rows(GROUP_SLOT), :]], axis=1))
-    mixed = dot(table, jnp.concatenate((high, high, low), axis=0))
-
-    def part(half, slot):
-        return mixed[half * PIECES : (half + 1) * PIECES, slot * ROWS : (slot + 1) * ROWS]
-
-    results = [
-        (part(0, slot) - part(1, slot + 1), part(1, slot) + part(0, slot + 1))
-        for slot in range(0, 2 * OWNED, 2)
-    ]
-    return results + [(part(0, GROUP_SLOT), part(1, GROUP_SLOT))]
+
+    def transform(values):
+        high, low = split(values)
+        mixed = dot(table, jnp.concatenate((high, high, low), axis=0))
+        return mixed[:PIECES], mixed[PIECES:]
+
+    taps = transform(rows[chip_rows(GROUP_SLOT), :])
+    results = []
+    for first in range(0, GROUP_SLOT, 2):
+        pair = [decode(rows[chip_rows(slot), :], scale_at(scales, slot)) for slot in (first, first + 1)]
+        cosines, sines = transform(jnp.concatenate(pair, axis=1))
+        results.append(
+            (cosines[:, :ROWS] - sines[:, ROWS:], sines[:, :ROWS] + cosines[:, ROWS:])
+        )
+    return results + [taps]
 
 
 def own_kernel(core_ref, in_ref, first_ref, out_ref, rows):
@@ -187,12 +189,14 @@
     )
     table = last_ref[core]
     last = jnp.concatenate((table[:, :PIECES], table[:, :PIECES], table[:, PIECES:]), axis=1)
-    twist_real, twist_imag = twist_ref[0], twist_ref[1]
-
-    def rotate(real, imag, sign):
+    twist_real, twist_imag = (
+        jnp.concatenate((twist_ref[i, :PIECES], sign * twist_ref[i, PIECES:]), axis=0) for i in range(2)
+    )
+
+    def rotate(real, imag, way):
         return (
-            real * twist_real - sign * (imag * twist_imag),
-            imag * twist_real + sign * (real * twist_imag),
+            real * twist_real - way * (imag * twist_imag),
+            imag * twist_real + way * (real * twist_imag),
         )
 
     def inner(real, imag):
@@ -203,7 +207,7 @@
     def both(index, part, other):
         column = (2 * index + part) * ROWS
         own = own_ref[:, column : column + ROWS]
-        return jnp.concatenate((own + other, sign * (own - other)), axis=0)
+        return jnp.concatenate((own + other, own - other), axis=0)
 
     def forward(index, real, imag):
         return inner(*rotate(both(index, 0, real), both(index, 1, imag), 1.0))
@@ -211,31 +215,36 @@
     def back(real, imag):
         turned_imag, turned_real = inner(imag, real)
         turned = jnp.concatenate(rotate(turned_real, turned_imag, -1.0), axis=1)
-        return turned[:PIECES] + sign * turned[PIECES:]
+        return turned[:PIECES] + turned[PIECES:]
 
     others = outer_forward(other_ref, rows, first_ref[1 - core])
     taps_real, taps_imag = forward(4, *others[4])
-    spectra = []
-    cross_real = cross_imag = None
-    for pair in range(2):
-        value_real, value_imag = forward(2 * pair, *others[2 * pair])
-        spectra.append(
-            back(
-                value_real * taps_real - value_imag * taps_imag,
-                value_real * taps_imag + value_imag * taps_real,
-            )
+
+    def with_taps(real, imag):
+        return back(
+            real * taps_real - imag * taps_imag,
+            real * taps_imag + imag * taps_real,
         )
-        grad_real, grad_imag = forward(2 * pair + 1, *others[2 * pair + 1])
-        spectra.append(
-            back(
-                grad_real * taps_real + grad_imag * taps_imag,
-                grad_imag * taps_real - grad_real * taps_imag,
-            )
+
+    def against_taps(real, imag):
+        return back(
+            real * taps_real + imag * taps_imag,
+            imag * taps_real - real * taps_imag,
         )
-        term_real = grad_real * value_real + grad_imag * value_imag
-        term_imag = grad_imag * value_real - grad_real * value_imag
-        cross_real = term_real if cross_real is None else cross_real + term_real
-        cross_imag = term_imag if cross_imag is None else cross_imag + term_imag
+
+    values, grads = [None] * 2, [None] * 2
+    values[0] = forward(0, *others[0])
+    grads[0] = forward(1, *others[1])
+    values[1] = forward(2, *others[2])
+    spectra = [with_taps(*values[0])]
+    grads[1] = forward(3, *others[3])
+    spectra.append(against_taps(*grads[0]))
+    spectra.append(with_taps(*values[1]))
+    spectra.append(against_taps(*grads[1]))
+    cross_real = cross_imag = 0.0
+    for (value_real, value_imag), (grad_real, grad_imag) in zip(values, grads):
+        cross_real = cross_real + (grad_real * value_real + grad_imag * value_imag)
+        cross_imag = cross_imag + (grad_imag * value_real - grad_real * value_imag)
     spectra.append(back(cross_real, cross_imag))
     high, low = split(jnp.concatenate(spectra, axis=1))
     final = dot(last, jnp.concatenate((high, low, high), axis=0))
@@ -248,7 +257,7 @@
         results.append(block(0, slot) + block(1, slot + 1))
         results.append(block(0, slot + 1) - block(1, slot))
     results.append(block(0, GROUP_SLOT) + block(1, GROUP_SLOT + 1))
-    scales = [scale_of(result) for result in results]
+    scales = [scale_of(result, axis=1) for result in results]
     for slot, result in enumerate(results):
         rows[chip_rows(slot), :] = encode(result, scales[slot])
     rows[chip_rows(SCALE_SLOT), :] = join_scales(

time: 51.7 us -> 51.4 us (level)
  no operation moved by 1% of the time
where the time goes in v5:
time: 51.4 us; the launch traced here: 51 us
  blocking collectives  42.4 us (82%)
  Pallas kernels  4.9 us (10%)
  starting transfers between devices  2.41 us (5%)
  between operations  0.71 us (1%)
  waiting for transfers between devices  0.56 us (1%)
    all_to_all x2, blocking collectives, exchange(): lax.all_to_all(blocks.reshape(CHIPS * SLOTS // 2, 2, ROWS), AXES, split_a...  42.4 us
    ppermute x1, starting transfers between devices, swap_cores(): return lax.ppermute(values, 'inner', [(i, i ^ 1) for i in range(count)])  2.41 us
    pallas_call x1, Pallas kernels, per_device(): pl.pallas_call(convolve_kernel, out_shape=packed, in_specs=[scalar] + [wh...  2.06 us
    pallas_call x1, Pallas kernels, per_device(): pl.pallas_call(pack_kernel, out_shape=packed, in_specs=[far] * 5, out_spe...  1.38 us
  transfers between devices with their start and end apart: 1, of which 1 were waited for; matrix products, arithmetic and copies ran while one was open for 0% of the time, Pallas kernels for 1%

profile of v5, /device:TPU:1, one launch (start us, length us, event | category | flops | bytes accessed | tf_op | source)
XLA Modules:
  0.0 51.0 jit_solution(2108361608784872054)
XLA Ops:
  0.6 1.4 %shard_map.128 = bf16[640,128]{1,0:T(8,128)(2,1)S(1)} custom-call(bf16[128,256]{1,0:T(8,128)(2,1)} %query_ref.3, bf16[128,256]{1,0:T(8,128)(2,1)} %key_ref.3, bf16[128,256]{1,0:T(8,128)(2,1)} %value_ref.3, bf16[16,128]{1,0:T(8,128)(2,1)} %taps_ref.1, bf16[128,256]{1,0:T(8,128)(2,1)} %upstream_ref.3), custom_call_target="tpu_custom_call" | custom-call | tf_op jit(solution)/shard_map/pallas_call | solution.py:355
  2.0 0.0 copy-start
  2.0 26.7 %all_to_all.10 = bf16[320,2,128]{2,1,0:T(2,128)(2,1)S(1)} all-to-all(bf16[320,2,128]{2,1,0:T(2,128)(2,1)S(1)} %bitcast.6), channel_id=1, replica_groups={{0,4,8,12,16,20,24,28,32,36,40,44,48,52,56,60,64,68,72,76,80,84,88,92,9..., dimensions={0} | all-to-all | bytes 327680 | tf_op jit(solution)/shard_map/all_to_all | solution.py:334
  28.7 2.4 %collective-permute-start = (bf16[640,128]{1,0:T(8,128)(2,1)S(1)}, bf16[640,128]{1,0:T(8,128)(2,1)S(1)}, u32[]{:S(2)}, u32[]{:S(2)}) collective-permute-start(bf16[640,128]{1,0:T(8,128)(2,1)S(1)} %bitcast.7), channel_id=1, source_target_pairs={{0,2},{2,0},{4,6},{6,4},{8,10},{10,8},{12,14},{14,12},{1,3},{3,1},... | collective-permute-start | bytes 491528 | tf_op jit(solution)/shard_map/ppermute | solution.py:329
  31.1 0.0 copy-done
  31.1 0.0 copy-start.1
  31.1 0.0 copy-start.2
  31.1 0.0 copy-start.7
  31.1 0.5 shard_map.129.own_ref
  31.6 0.6 %collective-permute-done.other_ref = bf16[640,128]{1,0:T(8,128)(2,1)S(1)} collective-permute-done((bf16[640,128]{1,0:T(8,128)(2,1)S(1)}, bf16[640,128]{1,0:T(8,128)(2,1)S(1)}, u32[]{:S(2)}, u32[]{:S(2)}) %collective-permute-start) | collective-permute-done | bytes 163872 | tf_op jit(solution)/shard_map/ppermute | solution.py:329
  32.2 0.0 copy-done.1
  32.2 0.0 copy-done.2
  32.2 0.0 copy-done.7
  32.2 2.1 %shard_map.130 = bf16[640,128]{1,0:T(8,128)(2,1)S(1)} custom-call(s32[1]{0:T(128)} %bitcast.core_ref, bf16[640,128]{1,0:T(8,128)(2,1)S(1)} %collective-permute-done.other_ref, f32[128,1280]{1,0:T(8,128)S(1)} %shard_map.129.own_ref, bf16[2,256,192]{2,1,0:T(8,128)(2,1)S(1)} %copy-done, bf16[512,256]{1,0:T(8,128)(2,1)S(1)} %copy-done.2, ...), custom_call_target="tpu_custom_call" | custom-call | tf_op jit(solution)/shard_map/pallas_call | solution.py:384
  34.3 0.0 copy-start.3
  34.3 0.0 copy-start.4
  34.3 0.0 copy-start.5
  34.3 0.0 copy-start.6
  34.3 15.7 %all_to_all.11 = bf16[320,2,128]{2,1,0:T(2,128)(2,1)S(1)} all-to-all(bf16[320,2,128]{2,1,0:T(2,128)(2,1)S(1)} %bitcast.9), channel_id=1, replica_groups={{0,4,8,12,16,20,24,28,32,36,40,44,48,52,56,60,64,68,72,76,80,84,88,92,9..., dimensions={0} | all-to-all | bytes 327680 | tf_op jit(solution)/shard_map/all_to_all | solution.py:334
  50.0 0.0 copy-done.3
  50.0 0.0 copy-done.4
  50.0 0.0 copy-done.5
  50.0 0.0 copy-done.6
  50.0 1.0 %shard_map.131 = (bf16[128,256]{1,0:T(8,128)(2,1)}, bf16[128,256]{1,0:T(8,128)(2,1)}, bf16[128,256]{1,0:T(8,128)(2,1)}, bf16[128,256]{1,0:T(8,128)(2,1)}, f32[16,128]{1,0:T(8,128)}) custom-call(bf16[640,128]{1,0:T(8,128)(2,1)S(1)} %bitcast.5, bf16[128,256]{1,0:T(8,128)(2,1)S(1)} %copy-done.3, bf16[128,256]{1,0:T(8,128)(2,1)S(1)} %copy-done.4, ...), custom_call_target="tpu_custom_call" | custom-call | tf_op jit(solution)/shard_map/pallas_call | solution.py:393
Async XLA Ops:
  2.0 29.1 %copy-start = (bf16[2,256,192]{2,1,0:T(8,128)(2,1)S(1)}, bf16[2,256,192]{2,1,0:T(8,128)(2,1)}, u32[]{:S(2)}) copy-start(bf16[2,256,192]{2,1,0:T(8,128)(2,1)} %constant.27.clone.first_ref) | copy-start | bytes 589828
  28.7 3.4 %collective-permute-start = (bf16[640,128]{1,0:T(8,128)(2,1)S(1)}, bf16[640,128]{1,0:T(8,128)(2,1)S(1)}, u32[]{:S(2)}, u32[]{:S(2)}) collective-permute-start(bf16[640,128]{1,0:T(8,128)(2,1)S(1)} %bitcast.7), channel_id=1, source_target_pairs={{0,2},{2,0},{4,6},{6,4},{8,10},{10,8},{12,14},{14,12},{1,3},{3,1},... | collective-permute-start | bytes 491528 | tf_op jit(solution)/shard_map/ppermute | solution.py:329
  31.1 1.0 %copy-start.1 = (f32[2,256,128]{2,1,0:T(8,128)S(1)}, f32[2,256,128]{2,1,0:T(8,128)}, u32[]{:S(2)}) copy-start(f32[2,256,128]{2,1,0:T(8,128)} %constant.29.clone.twist_ref) | copy-start | bytes 786436
  31.1 1.0 %copy-start.2 = (bf16[512,256]{1,0:T(8,128)(2,1)S(1)}, bf16[512,256]{1,0:T(8,128)(2,1)}, u32[]{:S(2)}) copy-start(bf16[512,256]{1,0:T(8,128)(2,1)} %constant.28.clone.second_ref) | copy-start | bytes 786436
  31.1 1.1 %copy-start.7 = (bf16[2,128,256]{2,1,0:T(8,128)(2,1)S(1)}, bf16[2,128,256]{2,1,0:T(8,128)(2,1)}, u32[]{:S(2)}) copy-start(bf16[2,128,256]{2,1,0:T(8,128)(2,1)} %constant.30.clone.last_ref) | copy-start | bytes 393220
  34.3 15.7 %copy-start.3 = (bf16[128,256]{1,0:T(8,128)(2,1)S(1)}, bf16[128,256]{1,0:T(8,128)(2,1)}, u32[]{:S(2)}) copy-start(bf16[128,256]{1,0:T(8,128)(2,1)} %query_ref.3) | copy-start | bytes 196612
  34.3 15.7 %copy-start.4 = (bf16[128,256]{1,0:T(8,128)(2,1)S(1)}, bf16[128,256]{1,0:T(8,128)(2,1)}, u32[]{:S(2)}) copy-start(bf16[128,256]{1,0:T(8,128)(2,1)} %key_ref.3) | copy-start | bytes 196612
  34.3 15.7 %copy-start.5 = (bf16[128,256]{1,0:T(8,128)(2,1)S(1)}, bf16[128,256]{1,0:T(8,128)(2,1)}, u32[]{:S(2)}) copy-start(bf16[128,256]{1,0:T(8,128)(2,1)} %value_ref.3) | copy-start | bytes 196612
  34.3 15.7 %copy-start.6 = (bf16[128,256]{1,0:T(8,128)(2,1)S(1)}, bf16[128,256]{1,0:T(8,128)(2,1)}, u32[]{:S(2)}) copy-start(bf16[128,256]{1,0:T(8,128)(2,1)} %upstream_ref.3) | copy-start | bytes 196612

commit v6 on v5

--- a/solution.py
+++ b/solution.py
@@ -136,13 +136,10 @@
                     array, pl.ds(SUBS * owned + sub, GROUPS, stride=GROUPS), :
                 ]
 
-    copies[0].wait()
-    copies[1].wait()
+    for copy in copies:
+        copy.wait()
     place(0, key, value)
-    copies[2].wait()
-    copies[3].wait()
     place(1, upstream, query)
-    copies[4].wait()
     for sub in range(SUBS):
         rows[chip_rows(GROUP_SLOT, GROUPS * sub, GROUPS), :] = taps[...].astype(F32)
         scales = [None] * GROUP_SLOT
@@ -286,13 +283,6 @@
     rows,
     sems,
 ):
-    copies = []
-
-    def send(source, target):
-        copy = pltpu.make_async_copy(source, target, sems.at[len(copies)])
-        copy.start()
-        copies.append(copy)
-
     rows[...] = in_ref[...].astype(F32)
     scales = rows[chip_rows(SCALE_SLOT), :]
 
@@ -306,20 +296,25 @@
                 ]
         return jnp.transpose(turned[array])
 
-    causal = collect(0)
-    mixed[...] = (query_ref[...].astype(F32) * causal).astype(BF16)
-    send(mixed, mixed_ref)
-    gquery[...] = (upstream_ref[...].astype(F32) * causal).astype(BF16)
-    send(gquery, gquery_ref)
-    back_conv = collect(1)
-    gkey[...] = (back_conv * value_ref[...].astype(F32)).astype(BF16)
-    send(gkey, gkey_ref)
-    gvalue[...] = (back_conv * key_ref[...].astype(F32)).astype(BF16)
-    send(gvalue, gvalue_ref)
     shares = decode(rows[chip_rows(GROUP_SLOT), :], scale_at(scales, GROUP_SLOT))
     parts = [shares[GROUPS * sub : GROUPS * (sub + 1)] for sub in range(SUBS)]
     gfilter[...] = (parts[0] + parts[1]) + (parts[2] + parts[3])
-    send(gfilter, gfilter_ref)
+    causal = collect(0)
+    back_conv = collect(1)
+    mixed[...] = (query_ref[...].astype(F32) * causal).astype(BF16)
+    gquery[...] = (upstream_ref[...].astype(F32) * causal).astype(BF16)
+    gkey[...] = (back_conv * value_ref[...].astype(F32)).astype(BF16)
+    gvalue[...] = (back_conv * key_ref[...].astype(F32)).astype(BF16)
+    moves = (
+        (mixed, mixed_ref),
+        (gquery, gquery_ref),
+        (gkey, gkey_ref),
+        (gvalue, gvalue_ref),
+        (gfilter, gfilter_ref),
+    )
+    copies = [pltpu.make_async_copy(a, b, sems.at[i]) for i, (a, b) in enumerate(moves)]
+    for copy in copies:
+        copy.start()
     for copy in copies:
         copy.wait()
 

time: 51.4 us -> 51.3 us (level)
  no operation moved by 1% of the time
where the time goes in v6:
time: 51.3 us; the launch traced here: 51 us
  blocking collectives  42.3 us (82%)
  Pallas kernels  4.88 us (10%)
  starting transfers between devices  2.41 us (5%)
  between operations  0.71 us (1%)
  waiting for transfers between devices  0.56 us (1%)
    all_to_all x2, blocking collectives, exchange(): lax.all_to_all(blocks.reshape(CHIPS * SLOTS // 2, 2, ROWS), AXES, split_a...  42.3 us
    ppermute x1, starting transfers between devices, swap_cores(): return lax.ppermute(values, 'inner', [(i, i ^ 1) for i in range(count)])  2.41 us
    pallas_call x1, Pallas kernels, per_device(): pl.pallas_call(convolve_kernel, out_shape=packed, in_specs=[scalar] + [wh...  2.07 us
    pallas_call x1, Pallas kernels, per_device(): pl.pallas_call(pack_kernel, out_shape=packed, in_specs=[far] * 5, out_spe...  1.34 us
  transfers between devices with their start and end apart: 1, of which 1 were waited for; matrix products, arithmetic and copies ran while one was open for 0% of the time, Pallas kernels for 1%

profile of v6, /device:TPU:1, one launch (start us, length us, event | category | flops | bytes accessed | tf_op | source)
XLA Modules:
  0.0 51.0 jit_solution(8761117375247788063)
XLA Ops:
  0.6 1.3 %shard_map.128 = bf16[640,128]{1,0:T(8,128)(2,1)S(1)} custom-call(bf16[128,256]{1,0:T(8,128)(2,1)} %query_ref.3, bf16[128,256]{1,0:T(8,128)(2,1)} %key_ref.3, bf16[128,256]{1,0:T(8,128)(2,1)} %value_ref.3, bf16[16,128]{1,0:T(8,128)(2,1)} %taps_ref.1, bf16[128,256]{1,0:T(8,128)(2,1)} %upstream_ref.3), custom_call_target="tpu_custom_call" | custom-call | tf_op jit(solution)/shard_map/pallas_call | solution.py:350
  2.0 0.0 copy-start
  2.0 26.7 %all_to_all.10 = bf16[320,2,128]{2,1,0:T(2,128)(2,1)S(1)} all-to-all(bf16[320,2,128]{2,1,0:T(2,128)(2,1)S(1)} %bitcast.6), channel_id=1, replica_groups={{0,4,8,12,16,20,24,28,32,36,40,44,48,52,56,60,64,68,72,76,80,84,88,92,9..., dimensions={0} | all-to-all | bytes 327680 | tf_op jit(solution)/shard_map/all_to_all | solution.py:329
  28.7 2.4 %collective-permute-start = (bf16[640,128]{1,0:T(8,128)(2,1)S(1)}, bf16[640,128]{1,0:T(8,128)(2,1)S(1)}, u32[]{:S(2)}, u32[]{:S(2)}) collective-permute-start(bf16[640,128]{1,0:T(8,128)(2,1)S(1)} %bitcast.7), channel_id=1, source_target_pairs={{0,2},{2,0},{4,6},{6,4},{8,10},{10,8},{12,14},{14,12},{1,3},{3,1},... | collective-permute-start | bytes 491528 | tf_op jit(solution)/shard_map/ppermute | solution.py:324
  31.1 0.0 copy-done
  31.1 0.0 copy-start.1
  31.1 0.0 copy-start.2
  31.1 0.0 copy-start.7
  31.1 0.4 shard_map.129.own_ref
  31.6 0.6 %collective-permute-done.other_ref = bf16[640,128]{1,0:T(8,128)(2,1)S(1)} collective-permute-done((bf16[640,128]{1,0:T(8,128)(2,1)S(1)}, bf16[640,128]{1,0:T(8,128)(2,1)S(1)}, u32[]{:S(2)}, u32[]{:S(2)}) %collective-permute-start) | collective-permute-done | bytes 163872 | tf_op jit(solution)/shard_map/ppermute | solution.py:324
  32.1 0.0 copy-done.1
  32.1 0.0 copy-done.2
  32.1 0.0 copy-done.7
  32.2 2.1 %shard_map.130 = bf16[640,128]{1,0:T(8,128)(2,1)S(1)} custom-call(s32[1]{0:T(128)} %bitcast.core_ref, bf16[640,128]{1,0:T(8,128)(2,1)S(1)} %collective-permute-done.other_ref, f32[128,1280]{1,0:T(8,128)S(1)} %shard_map.129.own_ref, bf16[2,256,192]{2,1,0:T(8,128)(2,1)S(1)} %copy-done, bf16[512,256]{1,0:T(8,128)(2,1)S(1)} %copy-done.2, ...), custom_call_target="tpu_custom_call" | custom-call | tf_op jit(solution)/shard_map/pallas_call | solution.py:379
  34.2 0.0 copy-start.3
  34.2 0.0 copy-start.4
  34.3 0.0 copy-start.5
  34.3 0.0 copy-start.6
  34.3 15.7 %all_to_all.11 = bf16[320,2,128]{2,1,0:T(2,128)(2,1)S(1)} all-to-all(bf16[320,2,128]{2,1,0:T(2,128)(2,1)S(1)} %bitcast.9), channel_id=1, replica_groups={{0,4,8,12,16,20,24,28,32,36,40,44,48,52,56,60,64,68,72,76,80,84,88,92,9..., dimensions={0} | all-to-all | bytes 327680 | tf_op jit(solution)/shard_map/all_to_all | solution.py:329
  49.9 0.0 copy-done.3
  49.9 0.0 copy-done.4
  49.9 0.0 copy-done.5
  49.9 0.0 copy-done.6
  50.0 1.0 %shard_map.131 = (bf16[128,256]{1,0:T(8,128)(2,1)}, bf16[128,256]{1,0:T(8,128)(2,1)}, bf16[128,256]{1,0:T(8,128)(2,1)}, bf16[128,256]{1,0:T(8,128)(2,1)}, f32[16,128]{1,0:T(8,128)}) custom-call(bf16[640,128]{1,0:T(8,128)(2,1)S(1)} %bitcast.5, bf16[128,256]{1,0:T(8,128)(2,1)S(1)} %copy-done.3, bf16[128,256]{1,0:T(8,128)(2,1)S(1)} %copy-done.4, ...), custom_call_target="tpu_custom_call" | custom-call | tf_op jit(solution)/shard_map/pallas_call | solution.py:388
Async XLA Ops:
  2.0 29.1 %copy-start = (bf16[2,256,192]{2,1,0:T(8,128)(2,1)S(1)}, bf16[2,256,192]{2,1,0:T(8,128)(2,1)}, u32[]{:S(2)}) copy-start(bf16[2,256,192]{2,1,0:T(8,128)(2,1)} %constant.27.clone.first_ref) | copy-start | bytes 589828
  28.7 3.4 %collective-permute-start = (bf16[640,128]{1,0:T(8,128)(2,1)S(1)}, bf16[640,128]{1,0:T(8,128)(2,1)S(1)}, u32[]{:S(2)}, u32[]{:S(2)}) collective-permute-start(bf16[640,128]{1,0:T(8,128)(2,1)S(1)} %bitcast.7), channel_id=1, source_target_pairs={{0,2},{2,0},{4,6},{6,4},{8,10},{10,8},{12,14},{14,12},{1,3},{3,1},... | collective-permute-start | bytes 491528 | tf_op jit(solution)/shard_map/ppermute | solution.py:324
  31.1 1.0 %copy-start.1 = (f32[2,256,128]{2,1,0:T(8,128)S(1)}, f32[2,256,128]{2,1,0:T(8,128)}, u32[]{:S(2)}) copy-start(f32[2,256,128]{2,1,0:T(8,128)} %constant.29.clone.twist_ref) | copy-start | bytes 786436
  31.1 1.0 %copy-start.2 = (bf16[512,256]{1,0:T(8,128)(2,1)S(1)}, bf16[512,256]{1,0:T(8,128)(2,1)}, u32[]{:S(2)}) copy-start(bf16[512,256]{1,0:T(8,128)(2,1)} %constant.28.clone.second_ref) | copy-start | bytes 786436
  31.1 1.1 %copy-start.7 = (bf16[2,128,256]{2,1,0:T(8,128)(2,1)S(1)}, bf16[2,128,256]{2,1,0:T(8,128)(2,1)}, u32[]{:S(2)}) copy-start(bf16[2,128,256]{2,1,0:T(8,128)(2,1)} %constant.30.clone.last_ref) | copy-start | bytes 393220
  34.2 15.7 %copy-start.3 = (bf16[128,256]{1,0:T(8,128)(2,1)S(1)}, bf16[128,256]{1,0:T(8,128)(2,1)}, u32[]{:S(2)}) copy-start(bf16[128,256]{1,0:T(8,128)(2,1)} %query_ref.3) | copy-start | bytes 196612
  34.2 15.7 %copy-start.4 = (bf16[128,256]{1,0:T(8,128)(2,1)S(1)}, bf16[128,256]{1,0:T(8,128)(2,1)}, u32[]{:S(2)}) copy-start(bf16[128,256]{1,0:T(8,128)(2,1)} %key_ref.3) | copy-start | bytes 196612
  34.3 15.7 %copy-start.5 = (bf16[128,256]{1,0:T(8,128)(2,1)S(1)}, bf16[128,256]{1,0:T(8,128)(2,1)}, u32[]{:S(2)}) copy-start(bf16[128,256]{1,0:T(8,128)(2,1)} %value_ref.3) | copy-start | bytes 196612
  34.3 15.7 %copy-start.6 = (bf16[128,256]{1,0:T(8,128)(2,1)S(1)}, bf16[128,256]{1,0:T(8,128)(2,1)}, u32[]{:S(2)}) copy-start(bf16[128,256]{1,0:T(8,128)(2,1)} %upstream_ref.3) | copy-start | bytes 196612

commit v7 on v6

--- a/solution.py
+++ b/solution.py
@@ -196,53 +196,47 @@
             imag * twist_real + way * (real * twist_imag),
         )
 
-    def inner(real, imag):
-        high, low = split(jnp.concatenate((real, imag), axis=1))
+    def inner(*sequences):
+        whole = jnp.concatenate([jnp.concatenate(parts, axis=1) for parts in sequences], axis=0)
+        high, low = split(whole)
         result = dot(jnp.concatenate((high, low, high), axis=1), second)
-        return result[:, :ROWS], result[:, ROWS:]
-
-    def both(index, part, other):
+        return [
+            (result[start : start + OUTER, :ROWS], result[start : start + OUTER, ROWS:])
+            for start in range(0, len(sequences) * OUTER, OUTER)
+        ]
+
+    def both(index, part):
         column = (2 * index + part) * ROWS
-        own = own_ref[:, column : column + ROWS]
+        own, other = own_ref[:, column : column + ROWS], others[index][part]
         return jnp.concatenate((own + other, own - other), axis=0)
 
-    def forward(index, real, imag):
-        return inner(*rotate(both(index, 0, real), both(index, 1, imag), 1.0))
-
-    def back(real, imag):
-        turned_imag, turned_real = inner(imag, real)
-        turned = jnp.concatenate(rotate(turned_real, turned_imag, -1.0), axis=1)
-        return turned[:PIECES] + turned[PIECES:]
+    def forward(*indices):
+        return inner(*(rotate(both(index, 0), both(index, 1), 1.0) for index in indices))
+
+    def back(*spectra):
+        halves = []
+        for turned_imag, turned_real in inner(*((imag, real) for real, imag in spectra)):
+            turned = jnp.concatenate(rotate(turned_real, turned_imag, -1.0), axis=1)
+            halves.append(turned[:PIECES] + turned[PIECES:])
+        return halves
 
     others = outer_forward(other_ref, rows, first_ref[1 - core])
-    taps_real, taps_imag = forward(4, *others[4])
+    ((taps_real, taps_imag),) = forward(4)
 
     def with_taps(real, imag):
-        return back(
-            real * taps_real - imag * taps_imag,
-            real * taps_imag + imag * taps_real,
-        )
+        return real * taps_real - imag * taps_imag, real * taps_imag + imag * taps_real
 
     def against_taps(real, imag):
-        return back(
-            real * taps_real + imag * taps_imag,
-            imag * taps_real - real * taps_imag,
-        )
-
-    values, grads = [None] * 2, [None] * 2
-    values[0] = forward(0, *others[0])
-    grads[0] = forward(1, *others[1])
-    values[1] = forward(2, *others[2])
-    spectra = [with_taps(*values[0])]
-    grads[1] = forward(3, *others[3])
-    spectra.append(against_taps(*grads[0]))
-    spectra.append(with_taps(*values[1]))
-    spectra.append(against_taps(*grads[1]))
+        return real * taps_real + imag * taps_imag, imag * taps_real - real * taps_imag
+
+    pairs = [forward(0, 1), forward(2, 3)]
+    spectra = []
     cross_real = cross_imag = 0.0
-    for (value_real, value_imag), (grad_real, grad_imag) in zip(values, grads):
-        cross_real = cross_real + (grad_real * value_real + grad_imag * value_imag)
-        cross_imag = cross_imag + (grad_imag * value_real - grad_real * value_imag)
-    spectra.append(back(cross_real, cross_imag))
+    for value, grad in pairs:
+        spectra += back(with_taps(*value), against_taps(*grad))
+        cross_real = cross_real + (grad[0] * value[0] + grad[1] * value[1])
+        cross_imag = cross_imag + (grad[1] * value[0] - grad[0] * value[1])
+    spectra += back((cross_real, cross_imag))
     high, low = split(jnp.concatenate(spectra, axis=1))
     final = dot(last, jnp.concatenate((high, low, high), axis=0))
 
@@ -274,14 +268,8 @@
     gkey_ref,
     gvalue_ref,
     gfilter_ref,
-    mixed,
-    gquery,
-    gkey,
-    gvalue,
-    gfilter,
     turned,
     rows,
-    sems,
 ):
     rows[...] = in_ref[...].astype(F32)
     scales = rows[chip_rows(SCALE_SLOT), :]
@@ -298,25 +286,13 @@
 
     shares = decode(rows[chip_rows(GROUP_SLOT), :], scale_at(scales, GROUP_SLOT))
     parts = [shares[GROUPS * sub : GROUPS * (sub + 1)] for sub in range(SUBS)]
-    gfilter[...] = (parts[0] + parts[1]) + (parts[2] + parts[3])
+    gfilter_ref[...] = (parts[0] + parts[1]) + (parts[2] + parts[3])
     causal = collect(0)
     back_conv = collect(1)
-    mixed[...] = (query_ref[...].astype(F32) * causal).astype(BF16)
-    gquery[...] = (upstream_ref[...].astype(F32) * causal).astype(BF16)
-    gkey[...] = (back_conv * value_ref[...].astype(F32)).astype(BF16)
-    gvalue[...] = (back_conv * key_ref[...].astype(F32)).astype(BF16)
-    moves = (
-        (mixed, mixed_ref),
-        (gquery, gquery_ref),
-        (gkey, gkey_ref),
-        (gvalue, gvalue_ref),
-        (gfilter, gfilter_ref),
-    )
-    copies = [pltpu.make_async_copy(a, b, sems.at[i]) for i, (a, b) in enumerate(moves)]
-    for copy in copies:
-        copy.start()
-    for copy in copies:
-        copy.wait()
+    mixed_ref[...] = (query_ref[...].astype(F32) * causal).astype(BF16)
+    gquery_ref[...] = (upstream_ref[...].astype(F32) * causal).astype(BF16)
+    gkey_ref[...] = (back_conv * value_ref[...].astype(F32)).astype(BF16)
+    gvalue_ref[...] = (back_conv * key_ref[...].astype(F32)).astype(BF16)
 
 
 def swap_cores(values):
@@ -389,17 +365,8 @@
         finish_kernel,
         out_shape=(out, out, out, out, jax.ShapeDtypeStruct((GROUPS, ROWS), F32)),
         in_specs=[whole] * 5,
-        out_specs=(far,) * 5,
-        scratch_shapes=[
-            wide,
-            wide,
-            wide,
-            wide,
-            pltpu.VMEM((GROUPS, ROWS), F32),
-            turned,
-            rows,
-            pltpu.SemaphoreType.DMA((5,)),
-        ],
+        out_specs=(whole,) * 5,
+        scratch_shapes=[turned, rows],
         compiler_params=small,
     )(exchange(results), gate_query, gate_key, value_input, grad_output)
 

time: 51.3 us -> 51.3 us (level)
  no operation moved by 1% of the time
where the time goes in v7:
time: 51.3 us; the launch traced here: 50.9 us
  blocking collectives  42.3 us (82%)
  Pallas kernels  4.8 us (9%)
  starting transfers between devices  2.41 us (5%)
  between operations  0.71 us (1%)
  waiting for transfers between devices  0.56 us (1%)
    all_to_all x2, blocking collectives, exchange(): lax.all_to_all(blocks.reshape(CHIPS * SLOTS // 2, 2, ROWS), AXES, split_a...  42.3 us
    ppermute x1, starting transfers between devices, swap_cores(): return lax.ppermute(values, 'inner', [(i, i ^ 1) for i in range(count)])  2.41 us
    pallas_call x1, Pallas kernels, per_device(): pl.pallas_call(convolve_kernel, out_shape=packed, in_specs=[scalar] + [wh...  2.03 us
    pallas_call x1, Pallas kernels, per_device(): pl.pallas_call(pack_kernel, out_shape=packed, in_specs=[far] * 5, out_spe...  1.34 us
  transfers between devices with their start and end apart: 1, of which 1 were waited for; matrix products, arithmetic and copies ran while one was open for 0% of the time, Pallas kernels for 1%

profile of v7, /device:TPU:1, one launch (start us, length us, event | category | flops | bytes accessed | tf_op | source)
XLA Modules:
  0.0 50.9 jit_solution(2407226662747840577)
XLA Ops:
  0.6 1.3 %shard_map.128 = bf16[640,128]{1,0:T(8,128)(2,1)S(1)} custom-call(bf16[128,256]{1,0:T(8,128)(2,1)} %query_ref.3, bf16[128,256]{1,0:T(8,128)(2,1)} %key_ref.3, bf16[128,256]{1,0:T(8,128)(2,1)} %value_ref.3, bf16[16,128]{1,0:T(8,128)(2,1)} %taps_ref.1, bf16[128,256]{1,0:T(8,128)(2,1)} %upstream_ref.3), custom_call_target="tpu_custom_call" | custom-call | tf_op jit(solution)/shard_map/pallas_call | solution.py:326
  2.0 0.0 copy-start
  2.0 26.7 %all_to_all.10 = bf16[320,2,128]{2,1,0:T(2,128)(2,1)S(1)} all-to-all(bf16[320,2,128]{2,1,0:T(2,128)(2,1)S(1)} %bitcast.6), channel_id=1, replica_groups={{0,4,8,12,16,20,24,28,32,36,40,44,48,52,56,60,64,68,72,76,80,84,88,92,9..., dimensions={0} | all-to-all | bytes 327680 | tf_op jit(solution)/shard_map/all_to_all | solution.py:305
  28.7 2.4 %collective-permute-start = (bf16[640,128]{1,0:T(8,128)(2,1)S(1)}, bf16[640,128]{1,0:T(8,128)(2,1)S(1)}, u32[]{:S(2)}, u32[]{:S(2)}) collective-permute-start(bf16[640,128]{1,0:T(8,128)(2,1)S(1)} %bitcast.7), channel_id=1, source_target_pairs={{0,2},{2,0},{4,6},{6,4},{8,10},{10,8},{12,14},{14,12},{1,3},{3,1},... | collective-permute-start | bytes 491528 | tf_op jit(solution)/shard_map/ppermute | solution.py:300
  31.1 0.0 copy-done
  31.1 0.0 copy-start.1
  31.1 0.0 copy-start.2
  31.1 0.0 copy-start.7
  31.1 0.4 shard_map.129.own_ref
  31.6 0.6 %collective-permute-done.other_ref = bf16[640,128]{1,0:T(8,128)(2,1)S(1)} collective-permute-done((bf16[640,128]{1,0:T(8,128)(2,1)S(1)}, bf16[640,128]{1,0:T(8,128)(2,1)S(1)}, u32[]{:S(2)}, u32[]{:S(2)}) %collective-permute-start) | collective-permute-done | bytes 163872 | tf_op jit(solution)/shard_map/ppermute | solution.py:300
  32.1 0.0 copy-done.1
  32.1 0.0 copy-done.2
  32.1 0.0 copy-done.7
  32.2 2.0 %shard_map.130 = bf16[640,128]{1,0:T(8,128)(2,1)S(1)} custom-call(s32[1]{0:T(128)} %bitcast.core_ref, bf16[640,128]{1,0:T(8,128)(2,1)S(1)} %collective-permute-done.other_ref, f32[128,1280]{1,0:T(8,128)S(1)} %shard_map.129.own_ref, bf16[2,256,192]{2,1,0:T(8,128)(2,1)S(1)} %copy-done, bf16[512,256]{1,0:T(8,128)(2,1)S(1)} %copy-done.2, ...), custom_call_target="tpu_custom_call" | custom-call | tf_op jit(solution)/shard_map/pallas_call | solution.py:355
  34.2 0.0 copy-start.3
  34.2 0.0 copy-start.4
  34.2 0.0 copy-start.5
  34.2 0.0 copy-start.6
  34.2 15.6 %all_to_all.11 = bf16[320,2,128]{2,1,0:T(2,128)(2,1)S(1)} all-to-all(bf16[320,2,128]{2,1,0:T(2,128)(2,1)S(1)} %bitcast.9), channel_id=1, replica_groups={{0,4,8,12,16,20,24,28,32,36,40,44,48,52,56,60,64,68,72,76,80,84,88,92,9..., dimensions={0} | all-to-all | bytes 327680 | tf_op jit(solution)/shard_map/all_to_all | solution.py:305
  49.9 0.0 copy-done.3
  49.9 0.0 copy-done.4
  49.9 0.0 copy-done.5
  49.9 0.0 copy-done.6
  49.9 1.0 %shard_map.131 = (bf16[128,256]{1,0:T(8,128)(2,1)}, bf16[128,256]{1,0:T(8,128)(2,1)}, bf16[128,256]{1,0:T(8,128)(2,1)}, bf16[128,256]{1,0:T(8,128)(2,1)}, f32[16,128]{1,0:T(8,128)}) custom-call(bf16[640,128]{1,0:T(8,128)(2,1)S(1)} %bitcast.5, bf16[128,256]{1,0:T(8,128)(2,1)S(1)} %copy-done.3, bf16[128,256]{1,0:T(8,128)(2,1)S(1)} %copy-done.4, ...), custom_call_target="tpu_custom_call" | custom-call | tf_op jit(solution)/shard_map/pallas_call | solution.py:364
Async XLA Ops:
  2.0 29.1 %copy-start = (bf16[2,256,192]{2,1,0:T(8,128)(2,1)S(1)}, bf16[2,256,192]{2,1,0:T(8,128)(2,1)}, u32[]{:S(2)}) copy-start(bf16[2,256,192]{2,1,0:T(8,128)(2,1)} %constant.27.clone.first_ref) | copy-start | bytes 589828
  28.7 3.4 %collective-permute-start = (bf16[640,128]{1,0:T(8,128)(2,1)S(1)}, bf16[640,128]{1,0:T(8,128)(2,1)S(1)}, u32[]{:S(2)}, u32[]{:S(2)}) collective-permute-start(bf16[640,128]{1,0:T(8,128)(2,1)S(1)} %bitcast.7), channel_id=1, source_target_pairs={{0,2},{2,0},{4,6},{6,4},{8,10},{10,8},{12,14},{14,12},{1,3},{3,1},... | collective-permute-start | bytes 491528 | tf_op jit(solution)/shard_map/ppermute | solution.py:300
  31.1 1.0 %copy-start.1 = (f32[2,256,128]{2,1,0:T(8,128)S(1)}, f32[2,256,128]{2,1,0:T(8,128)}, u32[]{:S(2)}) copy-start(f32[2,256,128]{2,1,0:T(8,128)} %constant.29.clone.twist_ref) | copy-start | bytes 786436
  31.1 1.0 %copy-start.2 = (bf16[512,256]{1,0:T(8,128)(2,1)S(1)}, bf16[512,256]{1,0:T(8,128)(2,1)}, u32[]{:S(2)}) copy-start(bf16[512,256]{1,0:T(8,128)(2,1)} %constant.28.clone.second_ref) | copy-start | bytes 786436
  31.1 1.1 %copy-start.7 = (bf16[2,128,256]{2,1,0:T(8,128)(2,1)S(1)}, bf16[2,128,256]{2,1,0:T(8,128)(2,1)}, u32[]{:S(2)}) copy-start(bf16[2,128,256]{2,1,0:T(8,128)(2,1)} %constant.30.clone.last_ref) | copy-start | bytes 393220
  34.2 15.7 %copy-start.3 = (bf16[128,256]{1,0:T(8,128)(2,1)S(1)}, bf16[128,256]{1,0:T(8,128)(2,1)}, u32[]{:S(2)}) copy-start(bf16[128,256]{1,0:T(8,128)(2,1)} %query_ref.3) | copy-start | bytes 196612
  34.2 15.7 %copy-start.4 = (bf16[128,256]{1,0:T(8,128)(2,1)S(1)}, bf16[128,256]{1,0:T(8,128)(2,1)}, u32[]{:S(2)}) copy-start(bf16[128,256]{1,0:T(8,128)(2,1)} %key_ref.3) | copy-start | bytes 196612
  34.2 15.7 %copy-start.5 = (bf16[128,256]{1,0:T(8,128)(2,1)S(1)}, bf16[128,256]{1,0:T(8,128)(2,1)}, u32[]{:S(2)}) copy-start(bf16[128,256]{1,0:T(8,128)(2,1)} %value_ref.3) | copy-start | bytes 196612
  34.2 15.7 %copy-start.6 = (bf16[128,256]{1,0:T(8,128)(2,1)S(1)}, bf16[128,256]{1,0:T(8,128)(2,1)}, u32[]{:S(2)}) copy-start(bf16[128,256]{1,0:T(8,128)(2,1)} %upstream_ref.3) | copy-start | bytes 196612

commit v8 on v7

--- a/solution.py
+++ b/solution.py
@@ -26,8 +26,8 @@
 RANGE = 125 / POWER
 REACH = 2.0 ** (2 * RANGE) - 1.0
 SHARE = 8
-SMALL = 4 * 1024 * 1024
-LARGE = 24 * 1024 * 1024
+SMALL = 2 * 1024 * 1024
+LARGE = 10 * 1024 * 1024
 F32 = jnp.float32
 BF16 = jnp.bfloat16
 
@@ -268,8 +268,14 @@
     gkey_ref,
     gvalue_ref,
     gfilter_ref,
+    mixed,
+    gquery,
+    gkey,
+    gvalue,
+    gfilter,
     turned,
     rows,
+    sems,
 ):
     rows[...] = in_ref[...].astype(F32)
     scales = rows[chip_rows(SCALE_SLOT), :]
@@ -286,13 +292,25 @@
 
     shares = decode(rows[chip_rows(GROUP_SLOT), :], scale_at(scales, GROUP_SLOT))
     parts = [shares[GROUPS * sub : GROUPS * (sub + 1)] for sub in range(SUBS)]
-    gfilter_ref[...] = (parts[0] + parts[1]) + (parts[2] + parts[3])
+    gfilter[...] = (parts[0] + parts[1]) + (parts[2] + parts[3])
     causal = collect(0)
     back_conv = collect(1)
-    mixed_ref[...] = (query_ref[...].astype(F32) * causal).astype(BF16)
-    gquery_ref[...] = (upstream_ref[...].astype(F32) * causal).astype(BF16)
-    gkey_ref[...] = (back_conv * value_ref[...].astype(F32)).astype(BF16)
-    gvalue_ref[...] = (back_conv * key_ref[...].astype(F32)).astype(BF16)
+    mixed[...] = (query_ref[...].astype(F32) * causal).astype(BF16)
+    gquery[...] = (upstream_ref[...].astype(F32) * causal).astype(BF16)
+    gkey[...] = (back_conv * value_ref[...].astype(F32)).astype(BF16)
+    gvalue[...] = (back_conv * key_ref[...].astype(F32)).astype(BF16)
+    moves = (
+        (mixed, mixed_ref),
+        (gquery, gquery_ref),
+        (gkey, gkey_ref),
+        (gvalue, gvalue_ref),
+        (gfilter, gfilter_ref),
+    )
+    copies = [pltpu.make_async_copy(a, b, sems.at[i]) for i, (a, b) in enumerate(moves)]
+    for copy in copies:
+        copy.start()
+    for copy in copies:
+        copy.wait()
 
 
 def swap_cores(values):
@@ -365,8 +383,17 @@
         finish_kernel,
         out_shape=(out, out, out, out, jax.ShapeDtypeStruct((GROUPS, ROWS), F32)),
         in_specs=[whole] * 5,
-        out_specs=(whole,) * 5,
-        scratch_shapes=[turned, rows],
+        out_specs=(far,) * 5,
+        scratch_shapes=[
+            wide,
+            wide,
+            wide,
+            wide,
+            pltpu.VMEM((GROUPS, ROWS), F32),
+            turned,
+            rows,
+            pltpu.SemaphoreType.DMA((5,)),
+        ],
         compiler_params=small,
     )(exchange(results), gate_query, gate_key, value_input, grad_output)
 

time: 51.3 us -> 51.3 us (level)
  no operation moved by 1% of the time
where the time goes in v8:
time: 51.3 us; the launch traced here: 50.9 us
  blocking collectives  42.3 us (82%)
  Pallas kernels  4.84 us (9%)
  starting transfers between devices  2.41 us (5%)
  between operations  0.71 us (1%)
  waiting for transfers between devices  0.56 us (1%)
    all_to_all x2, blocking collectives, exchange(): lax.all_to_all(blocks.reshape(CHIPS * SLOTS // 2, 2, ROWS), AXES, split_a...  42.3 us
    ppermute x1, starting transfers between devices, swap_cores(): return lax.ppermute(values, 'inner', [(i, i ^ 1) for i in range(count)])  2.41 us
    pallas_call x1, Pallas kernels, per_device(): pl.pallas_call(convolve_kernel, out_shape=packed, in_specs=[scalar] + [wh...  2.03 us
    pallas_call x1, Pallas kernels, per_device(): pl.pallas_call(pack_kernel, out_shape=packed, in_specs=[far] * 5, out_spe...  1.34 us
  transfers between devices with their start and end apart: 1, of which 1 were waited for; matrix products, arithmetic and copies ran while one was open for 0% of the time, Pallas kernels for 1%

profile of v8, /device:TPU:1, one launch (start us, length us, event | category | flops | bytes accessed | tf_op | source)
XLA Modules:
  0.0 50.9 jit_solution(12796154171189506065)
XLA Ops:
  0.6 1.3 %shard_map.128 = bf16[640,128]{1,0:T(8,128)(2,1)S(1)} custom-call(bf16[128,256]{1,0:T(8,128)(2,1)} %query_ref.3, bf16[128,256]{1,0:T(8,128)(2,1)} %key_ref.3, bf16[128,256]{1,0:T(8,128)(2,1)} %value_ref.3, bf16[16,128]{1,0:T(8,128)(2,1)} %taps_ref.1, bf16[128,256]{1,0:T(8,128)(2,1)} %upstream_ref.3), custom_call_target="tpu_custom_call" | custom-call | tf_op jit(solution)/shard_map/pallas_call | solution.py:344
  2.0 0.0 copy-start
  2.0 26.7 %all_to_all.10 = bf16[320,2,128]{2,1,0:T(2,128)(2,1)S(1)} all-to-all(bf16[320,2,128]{2,1,0:T(2,128)(2,1)S(1)} %bitcast.6), channel_id=1, replica_groups={{0,4,8,12,16,20,24,28,32,36,40,44,48,52,56,60,64,68,72,76,80,84,88,92,9..., dimensions={0} | all-to-all | bytes 327680 | tf_op jit(solution)/shard_map/all_to_all | solution.py:323
  28.7 2.4 %collective-permute-start = (bf16[640,128]{1,0:T(8,128)(2,1)S(1)}, bf16[640,128]{1,0:T(8,128)(2,1)S(1)}, u32[]{:S(2)}, u32[]{:S(2)}) collective-permute-start(bf16[640,128]{1,0:T(8,128)(2,1)S(1)} %bitcast.7), channel_id=1, source_target_pairs={{0,2},{2,0},{4,6},{6,4},{8,10},{10,8},{12,14},{14,12},{1,3},{3,1},... | collective-permute-start | bytes 491528 | tf_op jit(solution)/shard_map/ppermute | solution.py:318
  31.1 0.0 copy-done
  31.1 0.0 copy-start.1
  31.1 0.0 copy-start.2
  31.1 0.0 copy-start.7
  31.1 0.4 shard_map.129.own_ref
  31.6 0.6 %collective-permute-done.other_ref = bf16[640,128]{1,0:T(8,128)(2,1)S(1)} collective-permute-done((bf16[640,128]{1,0:T(8,128)(2,1)S(1)}, bf16[640,128]{1,0:T(8,128)(2,1)S(1)}, u32[]{:S(2)}, u32[]{:S(2)}) %collective-permute-start) | collective-permute-done | bytes 163872 | tf_op jit(solution)/shard_map/ppermute | solution.py:318
  32.1 0.0 copy-done.1
  32.1 0.0 copy-done.2
  32.1 0.0 copy-done.7
  32.2 2.0 %shard_map.130 = bf16[640,128]{1,0:T(8,128)(2,1)S(1)} custom-call(s32[1]{0:T(128)} %bitcast.core_ref, bf16[640,128]{1,0:T(8,128)(2,1)S(1)} %collective-permute-done.other_ref, f32[128,1280]{1,0:T(8,128)S(1)} %shard_map.129.own_ref, bf16[2,256,192]{2,1,0:T(8,128)(2,1)S(1)} %copy-done, bf16[512,256]{1,0:T(8,128)(2,1)S(1)} %copy-done.2, ...), custom_call_target="tpu_custom_call" | custom-call | tf_op jit(solution)/shard_map/pallas_call | solution.py:373
  34.2 0.0 copy-start.3
  34.2 0.0 copy-start.4
  34.2 0.0 copy-start.5
  34.2 0.0 copy-start.6
  34.2 15.6 %all_to_all.11 = bf16[320,2,128]{2,1,0:T(2,128)(2,1)S(1)} all-to-all(bf16[320,2,128]{2,1,0:T(2,128)(2,1)S(1)} %bitcast.9), channel_id=1, replica_groups={{0,4,8,12,16,20,24,28,32,36,40,44,48,52,56,60,64,68,72,76,80,84,88,92,9..., dimensions={0} | all-to-all | bytes 327680 | tf_op jit(solution)/shard_map/all_to_all | solution.py:323
  49.9 0.0 copy-done.3
  49.9 0.0 copy-done.4
  49.9 0.0 copy-done.5
  49.9 0.0 copy-done.6
  49.9 1.0 %shard_map.131 = (bf16[128,256]{1,0:T(8,128)(2,1)}, bf16[128,256]{1,0:T(8,128)(2,1)}, bf16[128,256]{1,0:T(8,128)(2,1)}, bf16[128,256]{1,0:T(8,128)(2,1)}, f32[16,128]{1,0:T(8,128)}) custom-call(bf16[640,128]{1,0:T(8,128)(2,1)S(1)} %bitcast.5, bf16[128,256]{1,0:T(8,128)(2,1)S(1)} %copy-done.3, bf16[128,256]{1,0:T(8,128)(2,1)S(1)} %copy-done.4, ...), custom_call_target="tpu_custom_call" | custom-call | tf_op jit(solution)/shard_map/pallas_call | solution.py:382
Async XLA Ops:
  2.0 29.1 %copy-start = (bf16[2,256,192]{2,1,0:T(8,128)(2,1)S(1)}, bf16[2,256,192]{2,1,0:T(8,128)(2,1)}, u32[]{:S(2)}) copy-start(bf16[2,256,192]{2,1,0:T(8,128)(2,1)} %constant.27.clone.first_ref) | copy-start | bytes 589828
  28.7 3.4 %collective-permute-start = (bf16[640,128]{1,0:T(8,128)(2,1)S(1)}, bf16[640,128]{1,0:T(8,128)(2,1)S(1)}, u32[]{:S(2)}, u32[]{:S(2)}) collective-permute-start(bf16[640,128]{1,0:T(8,128)(2,1)S(1)} %bitcast.7), channel_id=1, source_target_pairs={{0,2},{2,0},{4,6},{6,4},{8,10},{10,8},{12,14},{14,12},{1,3},{3,1},... | collective-permute-start | bytes 491528 | tf_op jit(solution)/shard_map/ppermute | solution.py:318
  31.1 1.0 %copy-start.1 = (f32[2,256,128]{2,1,0:T(8,128)S(1)}, f32[2,256,128]{2,1,0:T(8,128)}, u32[]{:S(2)}) copy-start(f32[2,256,128]{2,1,0:T(8,128)} %constant.29.clone.twist_ref) | copy-start | bytes 786436
  31.1 1.0 %copy-start.2 = (bf16[512,256]{1,0:T(8,128)(2,1)S(1)}, bf16[512,256]{1,0:T(8,128)(2,1)}, u32[]{:S(2)}) copy-start(bf16[512,256]{1,0:T(8,128)(2,1)} %constant.28.clone.second_ref) | copy-start | bytes 786436
  31.1 1.1 %copy-start.7 = (bf16[2,128,256]{2,1,0:T(8,128)(2,1)S(1)}, bf16[2,128,256]{2,1,0:T(8,128)(2,1)}, u32[]{:S(2)}) copy-start(bf16[2,128,256]{2,1,0:T(8,128)(2,1)} %constant.30.clone.last_ref) | copy-start | bytes 393220
  34.2 15.7 %copy-start.3 = (bf16[128,256]{1,0:T(8,128)(2,1)S(1)}, bf16[128,256]{1,0:T(8,128)(2,1)}, u32[]{:S(2)}) copy-start(bf16[128,256]{1,0:T(8,128)(2,1)} %query_ref.3) | copy-start | bytes 196612
  34.2 15.7 %copy-start.4 = (bf16[128,256]{1,0:T(8,128)(2,1)S(1)}, bf16[128,256]{1,0:T(8,128)(2,1)}, u32[]{:S(2)}) copy-start(bf16[128,256]{1,0:T(8,128)(2,1)} %key_ref.3) | copy-start | bytes 196612
  34.2 15.7 %copy-start.5 = (bf16[128,256]{1,0:T(8,128)(2,1)S(1)}, bf16[128,256]{1,0:T(8,128)(2,1)}, u32[]{:S(2)}) copy-start(bf16[128,256]{1,0:T(8,128)(2,1)} %value_ref.3) | copy-start | bytes 196612
  34.2 15.7 %copy-start.6 = (bf16[128,256]{1,0:T(8,128)(2,1)S(1)}, bf16[128,256]{1,0:T(8,128)(2,1)}, u32[]{:S(2)}) copy-start(bf16[128,256]{1,0:T(8,128)(2,1)} %upstream_ref.3) | copy-start | bytes 196612

commit v9 on v8

--- a/solution.py
+++ b/solution.py
@@ -237,11 +237,14 @@
         cross_real = cross_real + (grad[0] * value[0] + grad[1] * value[1])
         cross_imag = cross_imag + (grad[1] * value[0] - grad[0] * value[1])
     spectra += back((cross_real, cross_imag))
-    high, low = split(jnp.concatenate(spectra, axis=1))
-    final = dot(last, jnp.concatenate((high, low, high), axis=0))
+    finals = []
+    for spectrum in spectra:
+        high, low = split(spectrum)
+        finals.append(dot(last, jnp.concatenate((high, low, high), axis=0)))
 
     def block(half, index):
-        return final[half * CHIPS : (half + 1) * CHIPS, index * ROWS : (index + 1) * ROWS]
+        column = index % 2 * ROWS
+        return finals[index // 2][half * CHIPS : (half + 1) * CHIPS, column : column + ROWS]
 
     results = []
     for slot in range(0, GROUP_SLOT, 2):

time: 51.3 us -> 51.3 us (level)
  no operation moved by 1% of the time
where the time goes in v9:
time: 51.3 us; the launch traced here: 50.9 us
  blocking collectives  42.3 us (82%)
  Pallas kernels  4.84 us (9%)
  starting transfers between devices  2.41 us (5%)
  between operations  0.71 us (1%)
  waiting for transfers between devices  0.56 us (1%)
    all_to_all x2, blocking collectives, exchange(): lax.all_to_all(blocks.reshape(CHIPS * SLOTS // 2, 2, ROWS), AXES, split_a...  42.3 us
    ppermute x1, starting transfers between devices, swap_cores(): return lax.ppermute(values, 'inner', [(i, i ^ 1) for i in range(count)])  2.41 us
    pallas_call x1, Pallas kernels, per_device(): pl.pallas_call(convolve_kernel, out_shape=packed, in_specs=[scalar] + [wh...  2.03 us
    pallas_call x1, Pallas kernels, per_device(): pl.pallas_call(pack_kernel, out_shape=packed, in_specs=[far] * 5, out_spe...  1.34 us
  transfers between devices with their start and end apart: 1, of which 1 were waited for; matrix products, arithmetic and copies ran while one was open for 0% of the time, Pallas kernels for 1%

profile of v9, /device:TPU:1, one launch (start us, length us, event | category | flops | bytes accessed | tf_op | source)
XLA Modules:
  0.0 50.9 jit_solution(12796154171189506065)
XLA Ops:
  0.6 1.3 %shard_map.128 = bf16[640,128]{1,0:T(8,128)(2,1)S(1)} custom-call(bf16[128,256]{1,0:T(8,128)(2,1)} %query_ref.3, bf16[128,256]{1,0:T(8,128)(2,1)} %key_ref.3, bf16[128,256]{1,0:T(8,128)(2,1)} %value_ref.3, bf16[16,128]{1,0:T(8,128)(2,1)} %taps_ref.1, bf16[128,256]{1,0:T(8,128)(2,1)} %upstream_ref.3), custom_call_target="tpu_custom_call" | custom-call | tf_op jit(solution)/shard_map/pallas_call | solution.py:347
  2.0 0.0 copy-start
  2.0 26.7 %all_to_all.10 = bf16[320,2,128]{2,1,0:T(2,128)(2,1)S(1)} all-to-all(bf16[320,2,128]{2,1,0:T(2,128)(2,1)S(1)} %bitcast.6), channel_id=1, replica_groups={{0,4,8,12,16,20,24,28,32,36,40,44,48,52,56,60,64,68,72,76,80,84,88,92,9..., dimensions={0} | all-to-all | bytes 327680 | tf_op jit(solution)/shard_map/all_to_all | solution.py:326
  28.7 2.4 %collective-permute-start = (bf16[640,128]{1,0:T(8,128)(2,1)S(1)}, bf16[640,128]{1,0:T(8,128)(2,1)S(1)}, u32[]{:S(2)}, u32[]{:S(2)}) collective-permute-start(bf16[640,128]{1,0:T(8,128)(2,1)S(1)} %bitcast.7), channel_id=1, source_target_pairs={{0,2},{2,0},{4,6},{6,4},{8,10},{10,8},{12,14},{14,12},{1,3},{3,1},... | collective-permute-start | bytes 491528 | tf_op jit(solution)/shard_map/ppermute | solution.py:321
  31.1 0.0 copy-done
  31.1 0.0 copy-start.1
  31.1 0.0 copy-start.2
  31.1 0.0 copy-start.7
  31.1 0.4 shard_map.129.own_ref
  31.6 0.6 %collective-permute-done.other_ref = bf16[640,128]{1,0:T(8,128)(2,1)S(1)} collective-permute-done((bf16[640,128]{1,0:T(8,128)(2,1)S(1)}, bf16[640,128]{1,0:T(8,128)(2,1)S(1)}, u32[]{:S(2)}, u32[]{:S(2)}) %collective-permute-start) | collective-permute-done | bytes 163872 | tf_op jit(solution)/shard_map/ppermute | solution.py:321
  32.1 0.0 copy-done.1
  32.1 0.0 copy-done.2
  32.1 0.0 copy-done.7
  32.2 2.0 %shard_map.130 = bf16[640,128]{1,0:T(8,128)(2,1)S(1)} custom-call(s32[1]{0:T(128)} %bitcast.core_ref, bf16[640,128]{1,0:T(8,128)(2,1)S(1)} %collective-permute-done.other_ref, f32[128,1280]{1,0:T(8,128)S(1)} %shard_map.129.own_ref, bf16[2,256,192]{2,1,0:T(8,128)(2,1)S(1)} %copy-done, bf16[512,256]{1,0:T(8,128)(2,1)S(1)} %copy-done.2, ...), custom_call_target="tpu_custom_call" | custom-call | tf_op jit(solution)/shard_map/pallas_call | solution.py:376
  34.2 0.0 copy-start.3
  34.2 0.0 copy-start.4
  34.2 0.0 copy-start.5
  34.2 0.0 copy-start.6
  34.2 15.6 %all_to_all.11 = bf16[320,2,128]{2,1,0:T(2,128)(2,1)S(1)} all-to-all(bf16[320,2,128]{2,1,0:T(2,128)(2,1)S(1)} %bitcast.9), channel_id=1, replica_groups={{0,4,8,12,16,20,24,28,32,36,40,44,48,52,56,60,64,68,72,76,80,84,88,92,9..., dimensions={0} | all-to-all | bytes 327680 | tf_op jit(solution)/shard_map/all_to_all | solution.py:326
  49.9 0.0 copy-done.3
  49.9 0.0 copy-done.4
  49.9 0.0 copy-done.5
  49.9 0.0 copy-done.6
  49.9 1.0 %shard_map.131 = (bf16[128,256]{1,0:T(8,128)(2,1)}, bf16[128,256]{1,0:T(8,128)(2,1)}, bf16[128,256]{1,0:T(8,128)(2,1)}, bf16[128,256]{1,0:T(8,128)(2,1)}, f32[16,128]{1,0:T(8,128)}) custom-call(bf16[640,128]{1,0:T(8,128)(2,1)S(1)} %bitcast.5, bf16[128,256]{1,0:T(8,128)(2,1)S(1)} %copy-done.3, bf16[128,256]{1,0:T(8,128)(2,1)S(1)} %copy-done.4, ...), custom_call_target="tpu_custom_call" | custom-call | tf_op jit(solution)/shard_map/pallas_call | solution.py:385
Async XLA Ops:
  2.0 29.1 %copy-start = (bf16[2,256,192]{2,1,0:T(8,128)(2,1)S(1)}, bf16[2,256,192]{2,1,0:T(8,128)(2,1)}, u32[]{:S(2)}) copy-start(bf16[2,256,192]{2,1,0:T(8,128)(2,1)} %constant.27.clone.first_ref) | copy-start | bytes 589828
  28.7 3.4 %collective-permute-start = (bf16[640,128]{1,0:T(8,128)(2,1)S(1)}, bf16[640,128]{1,0:T(8,128)(2,1)S(1)}, u32[]{:S(2)}, u32[]{:S(2)}) collective-permute-start(bf16[640,128]{1,0:T(8,128)(2,1)S(1)} %bitcast.7), channel_id=1, source_target_pairs={{0,2},{2,0},{4,6},{6,4},{8,10},{10,8},{12,14},{14,12},{1,3},{3,1},... | collective-permute-start | bytes 491528 | tf_op jit(solution)/shard_map/ppermute | solution.py:321
  31.1 1.0 %copy-start.1 = (f32[2,256,128]{2,1,0:T(8,128)S(1)}, f32[2,256,128]{2,1,0:T(8,128)}, u32[]{:S(2)}) copy-start(f32[2,256,128]{2,1,0:T(8,128)} %constant.29.clone.twist_ref) | copy-start | bytes 786436
  31.1 1.0 %copy-start.2 = (bf16[512,256]{1,0:T(8,128)(2,1)S(1)}, bf16[512,256]{1,0:T(8,128)(2,1)}, u32[]{:S(2)}) copy-start(bf16[512,256]{1,0:T(8,128)(2,1)} %constant.28.clone.second_ref) | copy-start | bytes 786436
  31.1 1.1 %copy-start.7 = (bf16[2,128,256]{2,1,0:T(8,128)(2,1)S(1)}, bf16[2,128,256]{2,1,0:T(8,128)(2,1)}, u32[]{:S(2)}) copy-start(bf16[2,128,256]{2,1,0:T(8,128)(2,1)} %constant.30.clone.last_ref) | copy-start | bytes 393220
  34.2 15.7 %copy-start.3 = (bf16[128,256]{1,0:T(8,128)(2,1)S(1)}, bf16[128,256]{1,0:T(8,128)(2,1)}, u32[]{:S(2)}) copy-start(bf16[128,256]{1,0:T(8,128)(2,1)} %query_ref.3) | copy-start | bytes 196612
  34.2 15.7 %copy-start.4 = (bf16[128,256]{1,0:T(8,128)(2,1)S(1)}, bf16[128,256]{1,0:T(8,128)(2,1)}, u32[]{:S(2)}) copy-start(bf16[128,256]{1,0:T(8,128)(2,1)} %key_ref.3) | copy-start | bytes 196612
  34.2 15.7 %copy-start.5 = (bf16[128,256]{1,0:T(8,128)(2,1)S(1)}, bf16[128,256]{1,0:T(8,128)(2,1)}, u32[]{:S(2)}) copy-start(bf16[128,256]{1,0:T(8,128)(2,1)} %value_ref.3) | copy-start | bytes 196612
  34.2 15.7 %copy-start.6 = (bf16[128,256]{1,0:T(8,128)(2,1)S(1)}, bf16[128,256]{1,0:T(8,128)(2,1)}, u32[]{:S(2)}) copy-start(bf16[128,256]{1,0:T(8,128)(2,1)} %upstream_ref.3) | copy-start | bytes 196612

commit v10 on v9

--- a/solution.py
+++ b/solution.py
@@ -130,16 +130,17 @@
         turned[array] = jnp.transpose(codes).astype(F32)
         wide_scale = jnp.broadcast_to(scale.astype(BF16), (ROWS, CHANNELS))
         scaled[array] = jnp.transpose(wide_scale).astype(F32)
+
+    for copy in copies:
+        copy.wait()
+    place(0, key, value)
+    place(1, upstream, query)
+    for array in range(2):
         for owned in range(OWNED):
             for sub in range(SUBS):
                 rows[chip_rows(slot_of(array, owned), GROUPS * sub, GROUPS), :] = turned[
                     array, pl.ds(SUBS * owned + sub, GROUPS, stride=GROUPS), :
                 ]
-
-    for copy in copies:
-        copy.wait()
-    place(0, key, value)
-    place(1, upstream, query)
     for sub in range(SUBS):
         rows[chip_rows(GROUP_SLOT, GROUPS * sub, GROUPS), :] = taps[...].astype(F32)
         scales = [None] * GROUP_SLOT

time: 51.3 us -> 51.3 us (level)
  no operation moved by 1% of the time
where the time goes in v10:
time: 51.3 us; the launch traced here: 50.9 us
  blocking collectives  42.3 us (82%)
  Pallas kernels  4.84 us (9%)
  starting transfers between devices  2.41 us (5%)
  between operations  0.71 us (1%)
  waiting for transfers between devices  0.56 us (1%)
    all_to_all x2, blocking collectives, exchange(): lax.all_to_all(blocks.reshape(CHIPS * SLOTS // 2, 2, ROWS), AXES, split_a...  42.3 us
    ppermute x1, starting transfers between devices, swap_cores(): return lax.ppermute(values, 'inner', [(i, i ^ 1) for i in range(count)])  2.41 us
    pallas_call x1, Pallas kernels, per_device(): pl.pallas_call(convolve_kernel, out_shape=packed, in_specs=[scalar] + [wh...  2.03 us
    pallas_call x1, Pallas kernels, per_device(): pl.pallas_call(pack_kernel, out_shape=packed, in_specs=[far] * 5, out_spe...  1.34 us
  transfers between devices with their start and end apart: 1, of which 1 were waited for; matrix products, arithmetic and copies ran while one was open for 0% of the time, Pallas kernels for 1%

profile of v10, /device:TPU:1, one launch (start us, length us, event | category | flops | bytes accessed | tf_op | source)
XLA Modules:
  0.0 50.9 jit_solution(12796154171189506065)
XLA Ops:
  0.6 1.3 %shard_map.128 = bf16[640,128]{1,0:T(8,128)(2,1)S(1)} custom-call(bf16[128,256]{1,0:T(8,128)(2,1)} %query_ref.3, bf16[128,256]{1,0:T(8,128)(2,1)} %key_ref.3, bf16[128,256]{1,0:T(8,128)(2,1)} %value_ref.3, bf16[16,128]{1,0:T(8,128)(2,1)} %taps_ref.1, bf16[128,256]{1,0:T(8,128)(2,1)} %upstream_ref.3), custom_call_target="tpu_custom_call" | custom-call | tf_op jit(solution)/shard_map/pallas_call | solution.py:348
  2.0 0.0 copy-start
  2.0 26.7 %all_to_all.10 = bf16[320,2,128]{2,1,0:T(2,128)(2,1)S(1)} all-to-all(bf16[320,2,128]{2,1,0:T(2,128)(2,1)S(1)} %bitcast.6), channel_id=1, replica_groups={{0,4,8,12,16,20,24,28,32,36,40,44,48,52,56,60,64,68,72,76,80,84,88,92,9..., dimensions={0} | all-to-all | bytes 327680 | tf_op jit(solution)/shard_map/all_to_all | solution.py:327
  28.7 2.4 %collective-permute-start = (bf16[640,128]{1,0:T(8,128)(2,1)S(1)}, bf16[640,128]{1,0:T(8,128)(2,1)S(1)}, u32[]{:S(2)}, u32[]{:S(2)}) collective-permute-start(bf16[640,128]{1,0:T(8,128)(2,1)S(1)} %bitcast.7), channel_id=1, source_target_pairs={{0,2},{2,0},{4,6},{6,4},{8,10},{10,8},{12,14},{14,12},{1,3},{3,1},... | collective-permute-start | bytes 491528 | tf_op jit(solution)/shard_map/ppermute | solution.py:322
  31.1 0.0 copy-done
  31.1 0.0 copy-start.1
  31.1 0.0 copy-start.2
  31.1 0.0 copy-start.7
  31.1 0.4 shard_map.129.own_ref
  31.6 0.6 %collective-permute-done.other_ref = bf16[640,128]{1,0:T(8,128)(2,1)S(1)} collective-permute-done((bf16[640,128]{1,0:T(8,128)(2,1)S(1)}, bf16[640,128]{1,0:T(8,128)(2,1)S(1)}, u32[]{:S(2)}, u32[]{:S(2)}) %collective-permute-start) | collective-permute-done | bytes 163872 | tf_op jit(solution)/shard_map/ppermute | solution.py:322
  32.1 0.0 copy-done.1
  32.1 0.0 copy-done.2
  32.1 0.0 copy-done.7
  32.2 2.0 %shard_map.130 = bf16[640,128]{1,0:T(8,128)(2,1)S(1)} custom-call(s32[1]{0:T(128)} %bitcast.core_ref, bf16[640,128]{1,0:T(8,128)(2,1)S(1)} %collective-permute-done.other_ref, f32[128,1280]{1,0:T(8,128)S(1)} %shard_map.129.own_ref, bf16[2,256,192]{2,1,0:T(8,128)(2,1)S(1)} %copy-done, bf16[512,256]{1,0:T(8,128)(2,1)S(1)} %copy-done.2, ...), custom_call_target="tpu_custom_call" | custom-call | tf_op jit(solution)/shard_map/pallas_call | solution.py:377
  34.2 0.0 copy-start.3
  34.2 0.0 copy-start.4
  34.2 0.0 copy-start.5
  34.2 0.0 copy-start.6
  34.2 15.6 %all_to_all.11 = bf16[320,2,128]{2,1,0:T(2,128)(2,1)S(1)} all-to-all(bf16[320,2,128]{2,1,0:T(2,128)(2,1)S(1)} %bitcast.9), channel_id=1, replica_groups={{0,4,8,12,16,20,24,28,32,36,40,44,48,52,56,60,64,68,72,76,80,84,88,92,9..., dimensions={0} | all-to-all | bytes 327680 | tf_op jit(solution)/shard_map/all_to_all | solution.py:327
  49.9 0.0 copy-done.3
  49.9 0.0 copy-done.4
  49.9 0.0 copy-done.5
  49.9 0.0 copy-done.6
  49.9 1.0 %shard_map.131 = (bf16[128,256]{1,0:T(8,128)(2,1)}, bf16[128,256]{1,0:T(8,128)(2,1)}, bf16[128,256]{1,0:T(8,128)(2,1)}, bf16[128,256]{1,0:T(8,128)(2,1)}, f32[16,128]{1,0:T(8,128)}) custom-call(bf16[640,128]{1,0:T(8,128)(2,1)S(1)} %bitcast.5, bf16[128,256]{1,0:T(8,128)(2,1)S(1)} %copy-done.3, bf16[128,256]{1,0:T(8,128)(2,1)S(1)} %copy-done.4, ...), custom_call_target="tpu_custom_call" | custom-call | tf_op jit(solution)/shard_map/pallas_call | solution.py:386
Async XLA Ops:
  2.0 29.1 %copy-start = (bf16[2,256,192]{2,1,0:T(8,128)(2,1)S(1)}, bf16[2,256,192]{2,1,0:T(8,128)(2,1)}, u32[]{:S(2)}) copy-start(bf16[2,256,192]{2,1,0:T(8,128)(2,1)} %constant.27.clone.first_ref) | copy-start | bytes 589828
  28.7 3.4 %collective-permute-start = (bf16[640,128]{1,0:T(8,128)(2,1)S(1)}, bf16[640,128]{1,0:T(8,128)(2,1)S(1)}, u32[]{:S(2)}, u32[]{:S(2)}) collective-permute-start(bf16[640,128]{1,0:T(8,128)(2,1)S(1)} %bitcast.7), channel_id=1, source_target_pairs={{0,2},{2,0},{4,6},{6,4},{8,10},{10,8},{12,14},{14,12},{1,3},{3,1},... | collective-permute-start | bytes 491528 | tf_op jit(solution)/shard_map/ppermute | solution.py:322
  31.1 1.0 %copy-start.1 = (f32[2,256,128]{2,1,0:T(8,128)S(1)}, f32[2,256,128]{2,1,0:T(8,128)}, u32[]{:S(2)}) copy-start(f32[2,256,128]{2,1,0:T(8,128)} %constant.29.clone.twist_ref) | copy-start | bytes 786436
  31.1 1.0 %copy-start.2 = (bf16[512,256]{1,0:T(8,128)(2,1)S(1)}, bf16[512,256]{1,0:T(8,128)(2,1)}, u32[]{:S(2)}) copy-start(bf16[512,256]{1,0:T(8,128)(2,1)} %constant.28.clone.second_ref) | copy-start | bytes 786436
  31.1 1.1 %copy-start.7 = (bf16[2,128,256]{2,1,0:T(8,128)(2,1)S(1)}, bf16[2,128,256]{2,1,0:T(8,128)(2,1)}, u32[]{:S(2)}) copy-start(bf16[2,128,256]{2,1,0:T(8,128)(2,1)} %constant.30.clone.last_ref) | copy-start | bytes 393220
  34.2 15.7 %copy-start.3 = (bf16[128,256]{1,0:T(8,128)(2,1)S(1)}, bf16[128,256]{1,0:T(8,128)(2,1)}, u32[]{:S(2)}) copy-start(bf16[128,256]{1,0:T(8,128)(2,1)} %query_ref.3) | copy-start | bytes 196612
  34.2 15.7 %copy-start.4 = (bf16[128,256]{1,0:T(8,128)(2,1)S(1)}, bf16[128,256]{1,0:T(8,128)(2,1)}, u32[]{:S(2)}) copy-start(bf16[128,256]{1,0:T(8,128)(2,1)} %key_ref.3) | copy-start | bytes 196612
  34.2 15.7 %copy-start.5 = (bf16[128,256]{1,0:T(8,128)(2,1)S(1)}, bf16[128,256]{1,0:T(8,128)(2,1)}, u32[]{:S(2)}) copy-start(bf16[128,256]{1,0:T(8,128)(2,1)} %value_ref.3) | copy-start | bytes 196612
  34.2 15.7 %copy-start.6 = (bf16[128,256]{1,0:T(8,128)(2,1)S(1)}, bf16[128,256]{1,0:T(8,128)(2,1)}, u32[]{:S(2)}) copy-start(bf16[128,256]{1,0:T(8,128)(2,1)} %upstream_ref.3) | copy-start | bytes 196612
